TPU v7x, 512 devices: a whole 4x4x16 slice. The times are simulated.
512 devices in a mesh: span: 64 (over y, z), ctx: 8 (over x, core).
Axes of the slice: x: 4, y: 4, z: 16, core: 2. Of those that a mesh axis runs over, the one named last changes fastest.
Arguments:
- queries: bfloat16 [64, 8192], P('span')
- ctx_keys: bfloat16 [64, 2048, 1024], P('span', 'ctx'), may hold values from -6 to 6
- ctx_values: bfloat16 [64, 2048, 1024], P('span', 'ctx'), may hold values from -6 to 6
- lengths: int32 [64], P('span'), may hold values from 1 to 2048
- new_key: bfloat16 [64, 1024], P('span', 'ctx')
- new_value: bfloat16 [64, 1024], P('span', 'ctx'), may hold values from -6 to 6
- span_keys: bfloat16 [256, 512, 1024], P('span', None, 'ctx'), may hold values from -6 to 6
- span_values: bfloat16 [256, 512, 1024], P('span', None, 'ctx'), may hold values from -6 to 6
- span_lists: int32 [64, 16], P('span'), may hold values from 0 to 255, as said below
- span_slots: int32 [256], replicated, may hold values from 0 to 255, as said below
Outputs:
- attended: bfloat16 [64, 8192], P('span', 'ctx')
Inputs may be any that keep to these rules, and one draw needn't show every extreme that they name: `span_lists`: A slot s lies on index s // 4 of span, its holder. A request's 16 ids lie on 16 different holders; among the requests of one index of span, each holder is named at most once, and some holder exactly once. `span_slots`: each slot is named by exactly one id.
All inputs are finite; a program needn't handle non-finite values.
Results may differ from a plain program's by a relative error of at most 0.0095.
Values may be sent and summed in bfloat16 or wider, within the bound.
No kernel may reach another device: no remote copies, remote signals or barrier semaphores. Data moves between devices by JAX's collectives and lax.ppermute only.
A program may use at most 64 MiB of HBM per device.

v0:
```python
import jax
import jax.numpy as jnp
from jax import lax
from jax.sharding import PartitionSpec as P

HQ = 64
KVH = 8
DH = 128


def combined_all(value, axis, combine):
    everything = jax.tree.map(lambda part: lax.all_gather(part, axis), value)
    first = jax.tree.map(lambda part: part[0], everything)

    def step(k, so_far):
        return combine(so_far, jax.tree.map(lambda part: part[k], everything))

    return lax.fori_loop(1, lax.axis_size(axis), step, first)


def combine(first, second):
    numer_a, peak_a, total_a = first
    numer_b, peak_b, total_b = second
    highest = jnp.maximum(peak_a, peak_b)
    scale_a = jnp.exp(peak_a - highest)
    scale_b = jnp.exp(peak_b - highest)
    return (
        numer_a * scale_a[..., None] + numer_b * scale_b[..., None],
        highest,
        total_a * scale_a + total_b * scale_b,
    )


def shards(
    queries,
    ctx_keys,
    ctx_values,
    lengths,
    new_key,
    new_value,
    span_keys,
    span_values,
    span_lists,
    span_slots,
):
    req_dev, ctx_dev, kv_width = ctx_keys.shape
    kv_heads = kv_width // DH
    groups = new_key.shape[1] // DH
    per_group = HQ // KVH
    scaling = 1.0 / DH**0.5
    head_block = lax.axis_index("ctx")
    owner_index = lax.axis_index("span")
    query_all = queries.reshape(req_dev, kv_heads, per_group, DH)
    keys_priv = ctx_keys.reshape(req_dev, ctx_dev, kv_heads, DH)
    vals_priv = ctx_values.reshape(req_dev, ctx_dev, kv_heads, DH)
    scores = (
        jnp.einsum("rgqd,rpgd->rgqp", query_all, keys_priv, preferred_element_type=jnp.float32)
        * scaling
    )
    positions = head_block * ctx_dev + jnp.arange(ctx_dev, dtype=jnp.int32)
    valid = (positions[None, :] < lengths[:, None])[:, None, None, :]
    scores = jnp.where(valid, scores, -1e30)
    peak = jnp.max(scores, -1)
    weights = jnp.where(valid, jnp.exp(scores - peak[..., None]), 0.0)
    total = jnp.sum(weights, -1)
    numer = jnp.einsum("rgqp,rpgd->rgqd", weights, vals_priv, preferred_element_type=jnp.float32)
    merged_numer, merged_peak, merged_total = combined_all((numer, peak, total), "ctx", combine)
    start = head_block * groups
    private = (
        lax.dynamic_slice_in_dim(merged_numer, start, groups, 1),
        lax.dynamic_slice_in_dim(merged_peak, start, groups, 1),
        lax.dynamic_slice_in_dim(merged_total, start, groups, 1),
    )
    query_mine = lax.dynamic_slice_in_dim(
        queries, head_block * groups * per_group * DH, groups * per_group * DH, 1
    )
    gathered_query, gathered_lists = (
        lax.all_gather(query_mine, "span", axis=0, tiled=True),
        lax.all_gather(span_lists, "span", axis=0, tiled=True),
    )
    requests = gathered_query.shape[0]
    ch_dev = span_keys.shape[0]
    span_count = span_slots.shape[0]
    my_slots = owner_index * ch_dev + jnp.arange(ch_dev, dtype=jnp.int32)
    holder = span_slots[None, :] == my_slots[:, None]
    my_idents = jnp.sum(jnp.where(holder, jnp.arange(span_count, dtype=jnp.int32)[None, :], 0), 1)
    listed = jnp.any(gathered_lists[:, :, None] == my_idents[None, None, :], axis=1)
    query_group = gathered_query.reshape(requests, groups, per_group, DH)
    running = (
        jnp.zeros((requests, groups, per_group, DH), jnp.float32),
        jnp.full((requests, groups, per_group), -1e30, jnp.float32),
        jnp.zeros((requests, groups, per_group), jnp.float32),
    )
    for column in range(ch_dev):
        keys_span = span_keys[column].reshape(-1, groups, DH)
        vals_span = span_values[column].reshape(-1, groups, DH)
        span_scores = (
            jnp.einsum("rgqd,pgd->rgqp", query_group, keys_span, preferred_element_type=jnp.float32)
            * scaling
        )
        used = listed[:, column][:, None, None]
        span_peak = jnp.where(used, jnp.max(span_scores, -1), -1e30)
        span_weights = jnp.where(used[..., None], jnp.exp(span_scores - span_peak[..., None]), 0.0)
        span_total = jnp.sum(span_weights, -1)
        span_numer = jnp.einsum(
            "rgqp,pgd->rgqd", span_weights, vals_span, preferred_element_type=jnp.float32
        )
        running = combine(running, (span_numer, span_peak, span_total))
    run_numer, run_peak, run_total = running
    highest = lax.pmax(run_peak, "span")
    factor = jnp.exp(run_peak - highest)
    summed_numer, summed_total = (
        lax.psum_scatter(run_numer * factor[..., None], "span", scatter_dimension=0, tiled=True),
        lax.psum_scatter(run_total * factor, "span", scatter_dimension=0, tiled=True),
    )
    from_spans = (
        summed_numer,
        lax.dynamic_slice_in_dim(highest, owner_index * req_dev, req_dev, 0),
        summed_total,
    )
    query_own = query_mine.reshape(req_dev, groups, per_group, DH)
    key_own = new_key.reshape(req_dev, groups, DH)
    own_scores = (
        jnp.einsum("rgqd,rgd->rgq", query_own, key_own, preferred_element_type=jnp.float32)
        * scaling
    )
    own_numer = jnp.broadcast_to(
        new_value.reshape(req_dev, groups, 1, DH).astype(jnp.float32),
        (req_dev, groups, per_group, DH),
    )
    own_term = (own_numer, own_scores, jnp.ones_like(own_scores))
    final_numer, final_peak, final_total = combine(combine(private, from_spans), own_term)
    result = final_numer / final_total[..., None]
    return result.reshape(req_dev, groups * per_group * DH).astype(jnp.bfloat16)


def solution(mesh):
    in_specs = (
        P("span", None),
        P("span", "ctx", None),
        P("span", "ctx", None),
        P("span"),
        P("span", "ctx"),
        P("span", "ctx"),
        P("span", None, "ctx"),
        P("span", None, "ctx"),
        P("span", None),
        P(),
    )
    out_specs = P("span", "ctx")
    return jax.shard_map(shards, mesh=mesh, in_specs=in_specs, out_specs=out_specs, check_vma=False)
```

profile of v0, /device:TPU:6, one launch (start us, length us, event | category | flops | bytes accessed | tf_op | source)
XLA Modules:
  0.0 651.8 jit_solution(2028865947764223063)
XLA Ops:
  6.5 0.8 dynamic-slice_reduce_fusion
  7.3 88.9 %all-gather.4 = bf16[64,1,1024]{2,1,0:T(2,128)(2,1)S(1)} all-gather(bf16[1,1,1024]{2,1,0:T(2,128)(2,1)S(1)} %get-tuple-element.272), channel_id=1, replica_groups=mesh['span'=64,'ctx'=8] {'span'}, dimensions={0}, use_global_device_ids=true | all-gather | bytes 133120 | tf_op jit(solution)/shard_map/all_gather | solution.py:78
  96.2 0.8 reduce.13
  97.1 1.3 fusion.110
  98.4 0.4 fusion.111
  98.7 0.4 fusion.112
  99.1 1.3 fusion.113
  100.7 0.7 copy-done.8
  101.4 71.8 %all-gather.3 = s32[64,1,16]{2,1,0:T(1,128)S(1)} all-gather(s32[1,1,16]{2,1,0:T(1,128)S(1)} %bitcast.277), channel_id=1, replica_groups=mesh['span'=64,'ctx'=8] {'span'}, dimensions={0}, use_global_device_ids=true | all-gather | bytes 4160 | tf_op jit(solution)/shard_map/all_gather | solution.py:79
  173.2 0.7 copy-done.7
  173.9 0.2 select_reduce_fusion
  174.1 0.1 compare_reduce_fusion
  174.2 0.1 fusion.70
  174.3 140.3 %pmax.7 = f32[64,1,8]{0,2,1:T(8,128)S(1)} all-reduce(f32[64,1,8]{0,2,1:T(8,128)S(1)} %fusion.95), channel_id=1, replica_groups=mesh['span'=64,'ctx'=8] {'span'}, use_global_device_ids=true, to_apply=%region_10.11 | all-reduce | flops 512 | bytes 4096 | tf_op jit(solution)/shard_map/pmax | solution.py:110
  314.7 0.6 fusion.31
  315.4 1.8 fusion.29
  317.3 0.7 subtract_exponential_fusion.1
  318.0 0.7 copy.136
  318.8 1.8 fusion.20
  320.6 0.4 fusion.17
  321.0 0.4 fusion.14
  321.3 0.4 copy-done.6
  321.7 1.1 fusion.21
  322.8 0.7 copy-done.4
  323.5 0.1 reduce.12
  323.7 0.1 copy.149
  323.8 0.9 copy-done.2
  324.7 0.1 copy.148
  325.5 0.3 fusion.114
  325.8 12.8 %all-gather.1 = f32[64,8]{1,0:T(8,128)S(1)} all-gather(f32[8,8]{1,0:T(8,128)S(1)} %get-tuple-element.287), channel_id=3, replica_groups=mesh['span'=64,'ctx'=8] {'ctx'}, dimensions={0}, use_global_device_ids=true | all-gather | bytes 2304 | tf_op jit(solution)/shard_map/all_gather | solution.py:12
  338.6 0.2 fusion.64
  338.7 0.2 fusion.33
  339.0 12.8 %all-gather = f32[64,8,128]{2,1,0:T(8,128)S(1)} all-gather(f32[8,8,128]{2,1,0:T(8,128)S(1)} %fusion.33), channel_id=2, replica_groups=mesh['span'=64,'ctx'=8] {'ctx'}, dimensions={0}, use_global_device_ids=true | all-gather | bytes 294912 | tf_op jit(solution)/shard_map/all_gather | solution.py:12
  351.8 12.8 %all-gather.2 = f32[64,8]{1,0:T(8,128)S(1)} all-gather(f32[8,8]{1,0:T(8,128)S(1)} %fusion.64), channel_id=4, replica_groups=mesh['span'=64,'ctx'=8] {'ctx'}, dimensions={0}, use_global_device_ids=true | all-gather | bytes 2304 | tf_op jit(solution)/shard_map/all_gather | solution.py:12
  364.6 1.1 while.19
  364.6 0.1 fusion.124
  364.8 0.1 fusion.124
  365.0 0.1 fusion.124
  365.7 0.1 copy.130
  365.9 0.1 fusion.24
  366.1 274.0 %all-reduce.1 = f32[64,1,8]{2,1,0:T(1,128)S(1)} all-reduce(f32[64,1,8]{2,1,0:T(1,128)S(1)} %copy.144), channel_id=6, replica_groups=mesh['span'=64,'ctx'=8] {'span'}, use_global_device_ids=true, to_apply=%region_16.17.clone | all-reduce | flops 512 | bytes 4096
  640.1 1.3 dynamic-slice
  641.4 0.6 constant_dynamic-slice_fusion
  642.1 0.1 copy.139
  642.3 0.3 fusion.100
  642.5 0.4 copy-done.10
  642.9 1.4 fusion.99
  644.3 0.6 copy.159
  (66 shorter events, 1.6 us)
Async XLA Ops:
  6.5 359.3 %copy-start = (bf16[1,128]{1,0:T(2,128)(2,1)S(1)}, bf16[1,128]{1,0:T(2,128)(2,1)}, u32[]{:S(2)}) copy-start(bf16[1,128]{1,0:T(2,128)(2,1)} %param.16) | copy-start | bytes 772
  6.5 90.5 %copy-start.3 = (bf16[4,512,128]{2,1,0:T(8,128)(2,1)S(1)}, bf16[4,512,128]{2,1,0:T(8,128)(2,1)}, u32[]{:S(2)}) copy-start(bf16[4,512,128]{2,1,0:T(8,128)(2,1)} %param.18) | copy-start | bytes 1572868
  6.5 636.4 %all-reduce.4.cloned.1.call-start = ((), (), s32[]{:S(2)}) async-start(), calls=%async_computation | async-start | bytes 524288
  100.7 0.7 copy-start.8
  173.2 0.7 copy-start.7
  318.0 0.8 copy-start.5
  318.8 1.8 copy-start.9
  320.9 0.8 copy-start.6
  321.7 1.9 copy-start.1
  322.8 0.8 copy-start.4
  323.6 1.0 copy-start.2
  642.3 0.7 copy-start.10
Sparse Core Ops, SparseCore 0:
  322.9 251.1 all-reduce.3
where the time goes:
time: 652 us
  blocking collectives  613 us (94%)
  between operations  14.2 us (2%)
  local copies, waits for them, and re-layouts  9.13 us (1%)
  matrix products  7.62 us (1%)
  other arithmetic  7.02 us (1%)
    unnamed x1, blocking collectives  274 us
    pmax x1, blocking collectives, shards(): highest = lax.pmax(run_peak, 'span')  140 us
    all_gather x1, blocking collectives, shards(): lax.all_gather(query_mine, 'span', axis=0, tiled=True)  88.9 us
    all_gather x1, blocking collectives, shards(): lax.all_gather(span_lists, 'span', axis=0, tiled=True)  71.8 us
    all_gather x3, blocking collectives, combined_all(): everything = jax.tree.map(lambda part: lax.all_gather(part, axis), value)  38.4 us
  transfers between devices with their start and end apart: 1, of which 0 were waited for; matrix products, arithmetic and copies ran while one was open for 1% of the time, Pallas kernels for 0%

commit v1 on v0

v1 whole, which is shorter than its diff:
```python
import functools

import jax
import jax.numpy as jnp
from jax import lax
from jax.experimental import pallas as pl
from jax.experimental.pallas import tpu as pltpu
from jax.sharding import PartitionSpec as P

HQ = 64
KVH = 8
DH = 128
CORES = 2
LOW = -1e30
SCALE = 1.0 / DH**0.5
F32 = jnp.float32
BF16 = jnp.bfloat16


def swapped(value, mask):
    n = lax.axis_size("ctx")
    return lax.ppermute(value, "ctx", [(i, i ^ mask) for i in range(n)])


def exchanged(value):
    n = lax.axis_size("span")
    first = n * 7 // 16
    order = [(first + k) % n for k in range(n)]
    return lax.all_to_all(value, "span", 0, 0, axis_index_groups=[order], tiled=True)


def split(lse):
    high = lse.astype(BF16).astype(F32)
    rest = lse - high
    middle = rest.astype(BF16).astype(F32)
    return high, middle, rest - middle


def lanes(shape):
    return lax.broadcasted_iota(jnp.int32, shape, len(shape) - 1)


def spread(lse):
    lane = lanes(lse.shape[:-1] + (DH,))
    result = jnp.zeros(lane.shape, F32)
    for k, part in enumerate(split(lse)):
        result = jnp.where(lane == k, part, result)
    return result


def diagonals(shape):
    head = lax.broadcasted_iota(jnp.int32, shape, 1)
    return [lanes(shape) == head + 8 * k for k in range(3)]


def block_of(attended, lse):
    count = attended.shape[0]
    row = jnp.zeros(attended.shape, F32)
    for where, part in zip(diagonals(attended.shape), split(lse)):
        row = jnp.where(where, part, row)
    row = jnp.sum(row, 1, keepdims=True)
    row = jnp.broadcast_to(row, (count, 2, DH)).reshape(count, 1, 2, DH)
    return jnp.concatenate([attended.reshape(count, 4, 2, DH), row], 1).astype(BF16)


def fetch(pairs, sems):
    copies = [pltpu.make_async_copy(*pair, sems.at[k]) for k, pair in enumerate(pairs)]
    for copy in copies:
        copy.start()
    return copies


def pack_kernel(queries_ref, lists_ref, out_ref, held_ref, query_ref, ids_ref, sems):
    mine = lax.axis_index("ctx")
    width = KVH * DH
    part = queries_ref.at[:, pl.ds(pl.multiple_of(mine * width, width), width)]
    for copy in fetch(((part, query_ref), (lists_ref, ids_ref)), sems):
        copy.wait()
    query = query_ref[...].astype(F32)
    rows = [query[:, h * DH : (h + 1) * DH] for h in range(KVH)]
    ids = ids_ref[...].astype(F32)
    ids = jnp.concatenate([ids, jnp.full((1, DH - ids.shape[1]), -1.0, F32)], 1)
    block = jnp.concatenate(rows + [ids, ids], 0).reshape(5, 2, DH).astype(BF16)
    count = held_ref.shape[0]
    for copy in range(count):
        held_ref[copy] = block
    places = range(0, out_ref.shape[0], count)
    pairs = [(held_ref, out_ref.at[pl.ds(place, count)]) for place in places]
    for copy in fetch(pairs, sems):
        copy.wait()


def private_kernel(*refs):
    count = len(refs) // 2 - 2
    here_ref, there_ref, idents_ref = refs[count : count + 3]
    held, sems = refs[count + 3 : -1], refs[-1]
    copies = fetch(tuple(zip(refs[:count], held)), sems)
    lengths_ref, slots_ref, queries_ref, key_ref, value_ref, keys_ref, values_ref = held
    for copy in copies[:-1]:
        copy.wait()
    positions = keys_ref.shape[1]
    mine = lax.axis_index("ctx")
    first = mine * positions
    core = lax.rem(mine, CORES)
    chip = (mine - core) // CORES
    groups = [
        jnp.bitwise_xor(chip, step) * CORES + which
        for which in (core, 1 - core)
        for step in (0, 3, 1, 2)
    ]
    heads = [pl.ds(pl.multiple_of(g * DH, DH), DH) for g in groups]
    scores = []
    for k in range(KVH):
        width = 8 * DH
        mine_q = queries_ref[:, pl.ds(pl.multiple_of(groups[k] * width, width), width)]
        mine_q = mine_q.astype(F32)
        query = jnp.concatenate([mine_q[:, h * DH : (h + 1) * DH] for h in range(8)], 0)
        if k == 0:
            own = jnp.sum(query * key_ref[...].astype(F32), -1, keepdims=True) * SCALE
        scores.append(
            lax.dot_general(
                query.astype(BF16),
                keys_ref[0, :, heads[k]],
                (((1,), (1,)), ((), ())),
                preferred_element_type=F32,
            )
        )
    score = jnp.concatenate(scores, 0) * SCALE
    place = first + lax.broadcasted_iota(jnp.int32, score.shape, 1)
    valid = place < lengths_ref[0]
    score = jnp.where(valid, score, LOW)
    own = jnp.concatenate([own, jnp.full((HQ - 8, 1), LOW, F32)], 0)
    peak = jnp.maximum(jnp.max(score, -1, keepdims=True), own)
    weight = jnp.where(valid, jnp.exp(score - peak), 0.0)
    own = jnp.exp(own[:8] - peak[:8])
    total = jnp.sum(weight, -1, keepdims=True)
    total = jnp.concatenate([total[:8] + own, total[8:]], 0)
    some = total > 0.0
    safe = jnp.where(some, total, 1.0)
    stats = spread(jnp.where(some, peak + jnp.log(safe), LOW))
    weight = weight.astype(BF16)
    copies[-1].wait()
    for k in range(KVH):
        rows = slice(k * 8, k * 8 + 8)
        numer = jnp.dot(weight[rows], values_ref[0, :, heads[k]], preferred_element_type=F32)
        if k == 0:
            numer = numer + own * value_ref[...].astype(F32)
        message = jnp.concatenate([numer / safe[rows], stats[rows]], 0).astype(BF16)
        out_ref = here_ref if k < KVH // CORES else there_ref
        out_ref[k % (KVH // CORES)] = message
    table = slots_ref[...]
    number = (
        lax.broadcasted_iota(jnp.int32, table.shape, 0) * table.shape[1]
        + lax.broadcasted_iota(jnp.int32, table.shape, 1)
    )
    me = lax.axis_index("span")
    idents = []
    for column in range(idents_ref.shape[0]):
        found = jnp.where(table == me * idents_ref.shape[0] + column, number, 0)
        found = jnp.sum(jnp.sum(found, 0, keepdims=True), 1, keepdims=True)
        idents.append(jnp.broadcast_to(found, (1, DH)))
    idents_ref[...] = jnp.concatenate(idents, 0).astype(F32)


def span_kernel(gathered_ref, idents_ref, keys_ref, values_ref, out_ref):
    columns = keys_ref.shape[0]
    requests = gathered_ref.shape[0]
    count = min(32, requests)
    rows = count * 8
    keys = jnp.concatenate([keys_ref[column] for column in range(columns)], 1)
    values = jnp.concatenate([values_ref[column] for column in range(columns)], 1)
    for start in range(0, requests, count):
        message = gathered_ref[start : start + count].astype(F32)
        query = message[:, :4].reshape(rows, DH)
        ids = message[:, 4, :1, :]
        code = jnp.zeros_like(ids)
        for column in range(columns):
            ident = idents_ref[column : column + 1, :][None]
            code = jnp.where(ids == ident, column + 1.0, code)
        code = jnp.max(code, -1, keepdims=True)
        code = jnp.broadcast_to(code, (count, 8, DH)).reshape(rows, DH)
        listed = [code == column + 1.0 for column in range(columns)]
        query = jnp.concatenate([jnp.where(here, query, 0.0) for here in listed], 1)
        score = SCALE * lax.dot_general(
            query.astype(BF16), keys, (((1,), (1,)), ((), ())), preferred_element_type=F32
        )
        peak = jnp.max(score, -1, keepdims=True)
        weight = jnp.exp(score - peak)
        total = jnp.sum(weight, -1, keepdims=True)
        lse = jnp.where(code[:, :1] > 0.0, peak + jnp.log(total), LOW)
        numers = jnp.dot(weight.astype(BF16), values, preferred_element_type=F32)
        numer = jnp.zeros((rows, DH), F32)
        for column in range(columns):
            numer = jnp.where(listed[column], numers[:, column * DH : (column + 1) * DH], numer)
        attended = (numer / total).reshape(count, 8, DH)
        out_ref[start : start + count] = block_of(attended, lse.reshape(count, 8, 1))


def fold_kernel(first_ref, second_ref, *out_refs):
    parts = [first_ref[...].astype(F32), second_ref[...].astype(F32)]
    lses = [jnp.sum(part[:, 8:, :], -1, keepdims=True) for part in parts]
    peak = jnp.maximum(*lses)
    weights = [jnp.exp(lse - peak) for lse in lses]
    total = sum(weights)
    attended = sum(w * part[:, :8, :] for w, part in zip(weights, parts)) / total
    stats = spread(jnp.where(peak > LOW / 2, peak + jnp.log(total), LOW))
    result = jnp.concatenate([attended, stats], 1).astype(BF16)
    size = result.shape[0] // len(out_refs)
    for k, out_ref in enumerate(out_refs):
        out_ref[...] = result[k * size : (k + 1) * size]


def merge_kernel(spans_ref, here_ref, there_ref, out_ref):
    spans = spans_ref[...].astype(F32)
    attended = spans[:, :4].reshape(-1, 8, DH)
    row = jnp.broadcast_to(spans[:, 4, :1, :], attended.shape)
    kept = functools.reduce(jnp.logical_or, diagonals(attended.shape))
    lse = jnp.sum(jnp.where(kept, row, 0.0), -1, keepdims=True)
    tiles = [here_ref[0].astype(F32), there_ref[0].astype(F32)]
    lses = [jnp.sum(tile[8:], -1, keepdims=True) for tile in tiles]
    peak = functools.reduce(jnp.maximum, lses, jnp.max(lse, 0))
    weight = jnp.exp(lse - peak[None])
    weights = [jnp.exp(other - peak) for other in lses]
    total = sum(weights, jnp.sum(weight, 0))
    numer = sum(
        (w * tile[:8] for w, tile in zip(weights, tiles)), jnp.sum(weight * attended, 0)
    )
    result = numer / total
    out_ref[...] = jnp.concatenate([result[h : h + 1] for h in range(8)], 1).astype(BF16)


def vmem(count):
    return [pl.BlockSpec(memory_space=pltpu.VMEM)] * count


def hbm(count):
    return [pl.BlockSpec(memory_space=pltpu.HBM)] * count


def shards(
    queries,
    ctx_keys,
    ctx_values,
    lengths,
    new_key,
    new_value,
    span_keys,
    span_values,
    span_lists,
    span_slots,
):
    requests = lax.axis_size("span")
    chips = lax.axis_size("ctx") // CORES
    ch_dev = span_keys.shape[0]
    params = pltpu.CompilerParams(vmem_limit_bytes=16 * 1024 * 1024)
    alone = pltpu.CompilerParams(vmem_limit_bytes=56 * 1024 * 1024)
    blocks = jax.ShapeDtypeStruct((requests, 5, 2, DH), BF16)

    def tiles(count):
        return jax.ShapeDtypeStruct((count, 16, DH), BF16)

    def fold(here, there):
        return pl.pallas_call(
            fold_kernel,
            out_shape=[tiles(here.shape[0] // 2)] * 2,
            in_specs=vmem(2),
            out_specs=vmem(2),
            compiler_params=params,
            name="fold",
        )(here, there)

    packed = pl.pallas_call(
        pack_kernel,
        out_shape=blocks,
        in_specs=hbm(2),
        out_specs=hbm(1)[0],
        scratch_shapes=[
            pltpu.VMEM((requests // 4,) + blocks.shape[1:], BF16),
            pltpu.VMEM((1, KVH * DH), BF16),
            pltpu.VMEM(span_lists.shape, jnp.int32),
            pltpu.SemaphoreType.DMA((4,)),
        ],
        compiler_params=alone,
        name="pack",
    )(queries, span_lists)
    gathered = exchanged(packed)
    queries, packed = lax.optimization_barrier((queries, packed))
    table = span_slots.reshape(-1, min(DH, span_slots.shape[0]))
    fetched = (table, queries, new_key, new_value, ctx_keys, ctx_values)
    here, there, idents = pl.pallas_call(
        private_kernel,
        out_shape=[tiles(chips)] * CORES + [jax.ShapeDtypeStruct((ch_dev, DH), F32)],
        in_specs=hbm(1 + len(fetched)),
        out_specs=vmem(CORES + 1),
        scratch_shapes=[pltpu.SMEM(lengths.shape, jnp.int32)]
        + [pltpu.VMEM(array.shape, array.dtype) for array in fetched]
        + [pltpu.SemaphoreType.DMA((1 + len(fetched),))],
        compiler_params=alone,
        cost_estimate=pl.CostEstimate(
            flops=4 * HQ * ctx_keys.shape[1] * DH, bytes_accessed=1 << 20, transcendentals=1 << 14
        ),
        name="private",
    )(lengths, *fetched)
    there, gathered = lax.optimization_barrier((swapped(there, 1), gathered))
    partial = pl.pallas_call(
        span_kernel,
        out_shape=blocks,
        in_specs=vmem(4),
        out_specs=vmem(1)[0],
        compiler_params=params,
        cost_estimate=pl.CostEstimate(
            flops=4 * requests * 8 * DH * ch_dev * span_keys.shape[1],
            bytes_accessed=3 << 19,
            transcendentals=1 << 18,
        ),
        name="spans",
    )(gathered, idents, span_keys, span_values)
    partial = exchanged(partial)
    for mask in (1, 3):
        here, there = fold(here, there)
        there = swapped(there, mask * CORES)
    return pl.pallas_call(
        merge_kernel,
        out_shape=jax.ShapeDtypeStruct((1, KVH * DH), BF16),
        in_specs=vmem(3),
        out_specs=vmem(1)[0],
        compiler_params=params,
        name="merge",
    )(partial, here, there)


def solution(mesh):
    in_specs = (
        P("span", None),
        P("span", "ctx", None),
        P("span", "ctx", None),
        P("span"),
        P("span", "ctx"),
        P("span", "ctx"),
        P("span", None, "ctx"),
        P("span", None, "ctx"),
        P("span", None),
        P(),
    )
    out_specs = P("span", "ctx")
    return jax.shard_map(shards, mesh=mesh, in_specs=in_specs, out_specs=out_specs, check_vma=False)
```

time: 652 us -> 59.5 us (0.09)
  blocking collectives: 613 us -> 0 us
  starting transfers between devices: 0.01 us -> 36.8 us
  waiting for transfers between devices: 0.02 us -> 14.5 us
  between operations: 14.2 us -> 0.75 us
  local copies, waits for them, and re-layouts: 9.13 us -> 0.02 us
  matrix products: 7.62 us -> 0 us
  Pallas kernels: 0 us -> 7.13 us
  other arithmetic: 7.02 us -> 0 us
    unnamed x1 -> x0, blocking collectives: 274 us -> none
    all_gather x5 -> x0, blocking collectives: 199 us -> none  [the longest x1 88.9 us: shards(): lax.all_gather(query_mine, 'span', axis=0, tiled=True)]
    pmax x1 -> x0, blocking collectives: 140 us -> none  [shards(): highest = lax.pmax(run_peak, 'span')]
    all_to_all x0 -> x2, starting transfers between devices: none -> 29.7 us  [exchanged(): lax.all_to_all(value, 'span', 0, 0, axis_index_groups=[order], tiled=True)]
    ppermute x0 -> x3, waiting for transfers between devices: none -> 8.48 us  [swapped(): return lax.ppermute(value, 'ctx', [(i, i ^ mask) for i in range(n)])]
    dot_general x11 -> x0, matrix products: 7.62 us -> none  [the longest x4 3.6 us: shards(): jnp.einsum('rgqp,pgd->rgqd', span_weights, vals_span, preferred_element_t...]
    pallas_call x0 -> x6, Pallas kernels: none -> 7.13 us  [the longest x1 2.69 us: shards(): pl.pallas_call(private_kernel, out_shape=[tiles(chips)] * CORES + [jax.Sh...]
    ppermute x0 -> x3, starting transfers between devices: none -> 7.04 us  [swapped(): return lax.ppermute(value, 'ctx', [(i, i ^ mask) for i in range(n)])]
  transfers between devices with their start and end apart: 1 -> 5, of which waited for: 0 -> 4; matrix products, arithmetic and copies ran while one was open for 1% -> 0% of each run, Pallas kernels for 0% -> 5%
where the time goes in v1:
time: 59.5 us; the launch traced here: 59.1 us
  starting transfers between devices  36.8 us (62%)
  waiting for transfers between devices  14.5 us (24%)
  Pallas kernels  7.13 us (12%)
  between operations  0.75 us (1%)
    all_to_all x2, starting transfers between devices, exchanged(): lax.all_to_all(value, 'span', 0, 0, axis_index_groups=[order], tiled=True)  29.7 us
    ppermute x3, waiting for transfers between devices, swapped(): return lax.ppermute(value, 'ctx', [(i, i ^ mask) for i in range(n)])  8.48 us
    ppermute x3, starting transfers between devices, swapped(): return lax.ppermute(value, 'ctx', [(i, i ^ mask) for i in range(n)])  7.04 us
    all_to_all x2, waiting for transfers between devices, exchanged(): lax.all_to_all(value, 'span', 0, 0, axis_index_groups=[order], tiled=True)  5.99 us
    pallas_call x1, Pallas kernels, shards(): pl.pallas_call(private_kernel, out_shape=[tiles(chips)] * CORES + [jax.Sh...  2.69 us
    pallas_call x1, Pallas kernels, shards(): pl.pallas_call(span_kernel, out_shape=blocks, in_specs=vmem(4), out_specs...  1.97 us
    pallas_call x1, Pallas kernels, shards(): pl.pallas_call(pack_kernel, out_shape=blocks, in_specs=hbm(2), out_specs=...  1.42 us
  transfers between devices with their start and end apart: 5, of which 4 were waited for; matrix products, arithmetic and copies ran while one was open for 0% of the time, Pallas kernels for 5%

profile of v1, /device:TPU:6, one launch (start us, length us, event | category | flops | bytes accessed | tf_op | source)
XLA Modules:
  0.0 59.1 jit_solution(4370730074360711802)
XLA Ops:
  0.0 1.4 %pack.1 = bf16[64,5,2,128]{3,2,1,0:T(2,128)(2,1)} custom-call(bf16[1,8192]{1,0:T(2,128)(2,1)} %refs_2_, s32[1,16]{1,0:T(1,128)} %lists_ref.1), custom_call_target="tpu_custom_call" | custom-call | tf_op jit(solution)/shard_map/pack/pallas_call | solution.py:272
  1.4 19.1 %all-to-all-start = ((bf16[64,5,2,128]{3,2,1,0:T(2,128)(2,1)}), bf16[64,5,2,128]{3,2,1,0:T(2,128)(2,1)S(1)}, u32[]{:S(2)}, u32[]{:S(2)}) async-start(bf16[64,5,2,128]{3,2,1,0:T(2,128)(2,1)} %pack.1), calls=%async_computation | async-start | bytes 327680 | tf_op jit(solution)/shard_map/all_to_all | solution.py:29
  21.2 0.0 copy-start.1
  21.2 0.0 copy-start.2
  21.2 2.7 %private.1 = (bf16[4,16,128]{2,1,0:T(8,128)(2,1)}, bf16[4,16,128]{2,1,0:T(8,128)(2,1)}, f32[4,128]{1,0:T(4,128)}) custom-call(s32[1]{0:T(128)S(6)} %copy.11.refs_0_, s32[2,128]{1,0:T(2,128)} %bitcast.1, bf16[1,8192]{1,0:T(2,128)(2,1)} %refs_2_, bf16[1,128]{1,0:T(2,128)(2,1)} %refs_3_.1, bf16[1,128]{1,0:T(2,128)(2,1)} %refs_4_.1, ...), custom_call_target="tpu_custom_call" | custom-call | flops 8388608 | bytes 1048576 | tf_op jit(solution)/shard_map/private/pallas_call | solution.py:290
  23.9 0.0 copy-start.3
  23.9 1.9 %collective-permute-start = (bf16[4,16,128]{2,1,0:T(8,128)(2,1)}, bf16[4,16,128]{2,1,0:T(8,128)(2,1)S(1)}, u32[]{:S(2)}, u32[]{:S(2)}) collective-permute-start(bf16[4,16,128]{2,1,0:T(8,128)(2,1)} %get-tuple-element.16), channel_id=1, source_target_pairs={{0,1},{1,0},{2,3},{3,2},{4,5},{5,4},{6,7},{7,6},{8,9},{9,8},{10,11... | collective-permute-start | bytes 49160 | tf_op jit(solution)/shard_map/ppermute | solution.py:22
  25.8 1.4 %collective-permute-done.second_ref = bf16[4,16,128]{2,1,0:T(8,128)(2,1)S(1)} collective-permute-done((bf16[4,16,128]{2,1,0:T(8,128)(2,1)}, bf16[4,16,128]{2,1,0:T(8,128)(2,1)S(1)}, u32[]{:S(2)}, u32[]{:S(2)}) %collective-permute-start) | collective-permute-done | bytes 16416 | tf_op jit(solution)/shard_map/ppermute | solution.py:22
  27.2 6.0 %all-to-all-done.gathered_ref = bf16[64,5,2,128]{3,2,1,0:T(2,128)(2,1)S(1)} async-done(((bf16[64,5,2,128]{3,2,1,0:T(2,128)(2,1)}), bf16[64,5,2,128]{3,2,1,0:T(2,128)(2,1)S(1)}, u32[]{:S(2)}, u32[]{:S(2)}) %all-to-all-start) | async-done | bytes 163872 | tf_op jit(solution)/shard_map/all_to_all | solution.py:29
  33.2 0.0 copy-done.1
  33.2 0.0 copy-done.2
  33.2 0.0 copy-done.3
  33.2 2.0 %spans.1 = bf16[64,5,2,128]{3,2,1,0:T(2,128)(2,1)} custom-call(bf16[64,5,2,128]{3,2,1,0:T(2,128)(2,1)S(1)} %all-to-all-done.gathered_ref, f32[4,128]{1,0:T(4,128)S(1)} %copy-done.3, bf16[4,512,128]{2,1,0:T(8,128)(2,1)S(1)} %copy-done.1, bf16[4,512,128]{2,1,0:T(8,128)(2,1)S(1)} %copy-done.2), custom_call_target="tpu_custom_call" | custom-call | flops 536870912 | bytes 1572864 | tf_op jit(solution)/shard_map/spans/pallas_call | solution.py:305
  35.2 0.0 copy-start
  35.2 10.6 %all-to-all-start.1 = ((bf16[64,5,2,128]{3,2,1,0:T(2,128)(2,1)}), bf16[64,5,2,128]{3,2,1,0:T(2,128)(2,1)S(1)}, u32[]{:S(2)}, u32[]{:S(2)}) async-start(bf16[64,5,2,128]{3,2,1,0:T(2,128)(2,1)} %spans.1), calls=%async_computation.1 | async-start | bytes 327680 | tf_op jit(solution)/shard_map/all_to_all | solution.py:29
  45.8 0.0 copy-done
  45.8 0.1 fold.2
  45.9 2.7 %collective-permute-start.1 = (bf16[2,16,128]{2,1,0:T(8,128)(2,1)S(1)}, bf16[2,16,128]{2,1,0:T(8,128)(2,1)S(1)}, u32[]{:S(2)}, u32[]{:S(2)}) collective-permute-start(bf16[2,16,128]{2,1,0:T(8,128)(2,1)S(1)} %get-tuple-element.22), channel_id=1, source_target_pairs={{0,2},{1,3},{2,0},{3,1},{4,6},{5,7},{6,4},{7,5},{8,10},{9,11},{10,... | collective-permute-start | bytes 24584 | tf_op jit(solution)/shard_map/ppermute | solution.py:22
  48.7 2.8 %collective-permute-done.1.second_ref = bf16[2,16,128]{2,1,0:T(8,128)(2,1)S(1)} collective-permute-done((bf16[2,16,128]{2,1,0:T(8,128)(2,1)S(1)}, bf16[2,16,128]{2,1,0:T(8,128)(2,1)S(1)}, u32[]{:S(2)}, u32[]{:S(2)}) %collective-permute-start.1) | collective-permute-done | bytes 8224 | tf_op jit(solution)/shard_map/ppermute | solution.py:22
  51.5 0.1 fold.3
  51.6 2.4 %collective-permute-start.2 = (bf16[1,16,128]{2,1,0:T(8,128)(2,1)S(1)}, bf16[1,16,128]{2,1,0:T(8,128)(2,1)S(1)}, u32[]{:S(2)}, u32[]{:S(2)}) collective-permute-start(bf16[1,16,128]{2,1,0:T(8,128)(2,1)S(1)} %get-tuple-element.24), channel_id=1, source_target_pairs={{0,6},{1,7},{2,4},{3,5},{4,2},{5,3},{6,0},{7,1},{8,14},{9,15},{10,... | collective-permute-start | bytes 12296 | tf_op jit(solution)/shard_map/ppermute | solution.py:22
  54.0 4.3 %collective-permute-done.2.there_ref = bf16[1,16,128]{2,1,0:T(8,128)(2,1)S(1)} collective-permute-done((bf16[1,16,128]{2,1,0:T(8,128)(2,1)S(1)}, bf16[1,16,128]{2,1,0:T(8,128)(2,1)S(1)}, u32[]{:S(2)}, u32[]{:S(2)}) %collective-permute-start.2) | collective-permute-done | bytes 4128 | tf_op jit(solution)/shard_map/ppermute | solution.py:22
  58.3 0.0 all-to-all-done.1.spans_ref
  58.3 0.8 %merge.1 = bf16[1,1024]{1,0:T(2,128)(2,1)} custom-call(bf16[64,5,2,128]{3,2,1,0:T(2,128)(2,1)S(1)} %all-to-all-done.1.spans_ref, bf16[1,16,128]{2,1,0:T(8,128)(2,1)S(1)} %get-tuple-element.23.here_ref, bf16[1,16,128]{2,1,0:T(8,128)(2,1)S(1)} %collective-permute-done.2.there_ref), custom_call_target="tpu_custom_call" | custom-call | tf_op jit(solution)/shard_map/merge/pallas_call | solution.py:322
Async XLA Ops:
  1.4 31.8 %all-to-all-start = ((bf16[64,5,2,128]{3,2,1,0:T(2,128)(2,1)}), bf16[64,5,2,128]{3,2,1,0:T(2,128)(2,1)S(1)}, u32[]{:S(2)}, u32[]{:S(2)}) async-start(bf16[64,5,2,128]{3,2,1,0:T(2,128)(2,1)} %pack.1), calls=%async_computation | async-start | bytes 327680 | tf_op jit(solution)/shard_map/all_to_all | solution.py:29
  21.2 12.0 %copy-start.1 = (bf16[4,512,128]{2,1,0:T(8,128)(2,1)S(1)}, bf16[4,512,128]{2,1,0:T(8,128)(2,1)}, u32[]{:S(2)}) copy-start(bf16[4,512,128]{2,1,0:T(8,128)(2,1)} %keys_ref.1) | copy-start | bytes 1572868
  21.2 12.0 %copy-start.2 = (bf16[4,512,128]{2,1,0:T(8,128)(2,1)S(1)}, bf16[4,512,128]{2,1,0:T(8,128)(2,1)}, u32[]{:S(2)}) copy-start(bf16[4,512,128]{2,1,0:T(8,128)(2,1)} %values_ref.1) | copy-start | bytes 1572868
  23.9 9.3 %copy-start.3 = (f32[4,128]{1,0:T(4,128)S(1)}, f32[4,128]{1,0:T(4,128)}, u32[]{:S(2)}) copy-start(f32[4,128]{1,0:T(4,128)} %get-tuple-element.18.idents_ref) | copy-start | bytes 6148
  23.9 3.3 %collective-permute-start = (bf16[4,16,128]{2,1,0:T(8,128)(2,1)}, bf16[4,16,128]{2,1,0:T(8,128)(2,1)S(1)}, u32[]{:S(2)}, u32[]{:S(2)}) collective-permute-start(bf16[4,16,128]{2,1,0:T(8,128)(2,1)} %get-tuple-element.16), channel_id=1, source_target_pairs={{0,1},{1,0},{2,3},{3,2},{4,5},{5,4},{6,7},{7,6},{8,9},{9,8},{10,11... | collective-permute-start | bytes 49160 | tf_op jit(solution)/shard_map/ppermute | solution.py:22
  35.2 10.6 %copy-start = (bf16[4,16,128]{2,1,0:T(8,128)(2,1)S(1)}, bf16[4,16,128]{2,1,0:T(8,128)(2,1)}, u32[]{:S(2)}) copy-start(bf16[4,16,128]{2,1,0:T(8,128)(2,1)} %get-tuple-element.19.first_ref) | copy-start | bytes 49156
  35.2 23.1 %all-to-all-start.1 = ((bf16[64,5,2,128]{3,2,1,0:T(2,128)(2,1)}), bf16[64,5,2,128]{3,2,1,0:T(2,128)(2,1)S(1)}, u32[]{:S(2)}, u32[]{:S(2)}) async-start(bf16[64,5,2,128]{3,2,1,0:T(2,128)(2,1)} %spans.1), calls=%async_computation.1 | async-start | bytes 327680 | tf_op jit(solution)/shard_map/all_to_all | solution.py:29
  45.9 5.5 %collective-permute-start.1 = (bf16[2,16,128]{2,1,0:T(8,128)(2,1)S(1)}, bf16[2,16,128]{2,1,0:T(8,128)(2,1)S(1)}, u32[]{:S(2)}, u32[]{:S(2)}) collective-permute-start(bf16[2,16,128]{2,1,0:T(8,128)(2,1)S(1)} %get-tuple-element.22), channel_id=1, source_target_pairs={{0,2},{1,3},{2,0},{3,1},{4,6},{5,7},{6,4},{7,5},{8,10},{9,11},{10,... | collective-permute-start | bytes 24584 | tf_op jit(solution)/shard_map/ppermute | solution.py:22
  51.6 6.7 %collective-permute-start.2 = (bf16[1,16,128]{2,1,0:T(8,128)(2,1)S(1)}, bf16[1,16,128]{2,1,0:T(8,128)(2,1)S(1)}, u32[]{:S(2)}, u32[]{:S(2)}) collective-permute-start(bf16[1,16,128]{2,1,0:T(8,128)(2,1)S(1)} %get-tuple-element.24), channel_id=1, source_target_pairs={{0,6},{1,7},{2,4},{3,5},{4,2},{5,3},{6,0},{7,1},{8,14},{9,15},{10,... | collective-permute-start | bytes 12296 | tf_op jit(solution)/shard_map/ppermute | solution.py:22

commit v2 on v1

--- a/solution.py
+++ b/solution.py
@@ -13,6 +13,7 @@
 CORES = 2
 LOW = -1e30
 SCALE = 1.0 / DH**0.5
+LOG2E = 1.4426950408889634
 F32 = jnp.float32
 BF16 = jnp.bfloat16
 
@@ -162,32 +163,36 @@
     idents_ref[...] = jnp.concatenate(idents, 0).astype(F32)
 
 
+def turn_kernel(keys_ref, out_ref):
+    size = keys_ref.shape[2]
+    for column in range(keys_ref.shape[0]):
+        turned = keys_ref[column].astype(F32).T
+        out_ref[column * size : (column + 1) * size, :] = turned.astype(BF16)
+
+
 def span_kernel(gathered_ref, idents_ref, keys_ref, values_ref, out_ref):
-    columns = keys_ref.shape[0]
+    columns = values_ref.shape[0]
     requests = gathered_ref.shape[0]
     count = min(32, requests)
     rows = count * 8
-    keys = jnp.concatenate([keys_ref[column] for column in range(columns)], 1)
     values = jnp.concatenate([values_ref[column] for column in range(columns)], 1)
     for start in range(0, requests, count):
         message = gathered_ref[start : start + count].astype(F32)
         query = message[:, :4].reshape(rows, DH)
-        ids = message[:, 4, :1, :]
+        ids = message[:, 4, 0, :]
         code = jnp.zeros_like(ids)
         for column in range(columns):
-            ident = idents_ref[column : column + 1, :][None]
-            code = jnp.where(ids == ident, column + 1.0, code)
+            code = jnp.where(ids == idents_ref[column : column + 1, :], column + 1.0, code)
         code = jnp.max(code, -1, keepdims=True)
-        code = jnp.broadcast_to(code, (count, 8, DH)).reshape(rows, DH)
+        code = jnp.broadcast_to(code[:, None, :], (count, 8, DH)).reshape(rows, DH)
         listed = [code == column + 1.0 for column in range(columns)]
         query = jnp.concatenate([jnp.where(here, query, 0.0) for here in listed], 1)
-        score = SCALE * lax.dot_general(
-            query.astype(BF16), keys, (((1,), (1,)), ((), ())), preferred_element_type=F32
-        )
+        score = jnp.dot(query.astype(BF16), keys_ref[...], preferred_element_type=F32)
+        score = score * (SCALE * LOG2E)
         peak = jnp.max(score, -1, keepdims=True)
-        weight = jnp.exp(score - peak)
+        weight = jnp.exp2(score - peak)
         total = jnp.sum(weight, -1, keepdims=True)
-        lse = jnp.where(code[:, :1] > 0.0, peak + jnp.log(total), LOW)
+        lse = jnp.where(code[:, :1] > 0.0, peak * (1.0 / LOG2E) + jnp.log(total), LOW)
         numers = jnp.dot(weight.astype(BF16), values, preferred_element_type=F32)
         numer = jnp.zeros((rows, DH), F32)
         for column in range(columns):
@@ -284,7 +289,7 @@
         name="pack",
     )(queries, span_lists)
     gathered = exchanged(packed)
-    queries, packed = lax.optimization_barrier((queries, packed))
+    queries, span_keys, packed = lax.optimization_barrier((queries, span_keys, packed))
     table = span_slots.reshape(-1, min(DH, span_slots.shape[0]))
     fetched = (table, queries, new_key, new_value, ctx_keys, ctx_values)
     here, there, idents = pl.pallas_call(
@@ -302,6 +307,14 @@
         name="private",
     )(lengths, *fetched)
     there, gathered = lax.optimization_barrier((swapped(there, 1), gathered))
+    turned = pl.pallas_call(
+        turn_kernel,
+        out_shape=jax.ShapeDtypeStruct((ch_dev * DH, span_keys.shape[1]), BF16),
+        in_specs=vmem(1),
+        out_specs=vmem(1)[0],
+        compiler_params=params,
+        name="turn",
+    )(span_keys)
     partial = pl.pallas_call(
         span_kernel,
         out_shape=blocks,
@@ -314,7 +327,7 @@
             transcendentals=1 << 18,
         ),
         name="spans",
-    )(gathered, idents, span_keys, span_values)
+    )(gathered, idents, turned, span_values)
     partial = exchanged(partial)
     for mask in (1, 3):
         here, there = fold(here, there)

time: 59.5 us -> 59.5 us (level)
  no operation moved by 1% of the time
where the time goes in v2:
time: 59.5 us; the launch traced here: 59.1 us
  starting transfers between devices  36.9 us (62%)
  waiting for transfers between devices  14.1 us (24%)
  Pallas kernels  7.3 us (12%)
  between operations  0.77 us (1%)
    all_to_all x2, starting transfers between devices, exchanged(): lax.all_to_all(value, 'span', 0, 0, axis_index_groups=[order], tiled=True)  29.7 us
    ppermute x3, waiting for transfers between devices, swapped(): return lax.ppermute(value, 'ctx', [(i, i ^ mask) for i in range(n)])  8.24 us
    ppermute x3, starting transfers between devices, swapped(): return lax.ppermute(value, 'ctx', [(i, i ^ mask) for i in range(n)])  7.19 us
    all_to_all x2, waiting for transfers between devices, exchanged(): lax.all_to_all(value, 'span', 0, 0, axis_index_groups=[order], tiled=True)  5.89 us
    pallas_call x1, Pallas kernels, shards(): pl.pallas_call(private_kernel, out_shape=[tiles(chips)] * CORES + [jax.Sh...  2.67 us
    pallas_call x1, Pallas kernels, shards(): pl.pallas_call(span_kernel, out_shape=blocks, in_specs=vmem(4), out_specs...  1.95 us
    pallas_call x1, Pallas kernels, shards(): pl.pallas_call(pack_kernel, out_shape=blocks, in_specs=hbm(2), out_specs=...  1.42 us
  transfers between devices with their start and end apart: 5, of which 4 were waited for; matrix products, arithmetic and copies ran while one was open for 0% of the time, Pallas kernels for 5%

profile of v2, /device:TPU:6, one launch (start us, length us, event | category | flops | bytes accessed | tf_op | source)
XLA Modules:
  0.0 59.1 jit_solution(1569636185832167202)
XLA Ops:
  0.0 1.4 %pack.1 = bf16[64,5,2,128]{3,2,1,0:T(2,128)(2,1)} custom-call(bf16[1,8192]{1,0:T(2,128)(2,1)} %refs_2_, s32[1,16]{1,0:T(1,128)} %lists_ref.1), custom_call_target="tpu_custom_call" | custom-call | tf_op jit(solution)/shard_map/pack/pallas_call | solution.py:277
  1.4 19.1 %all-to-all-start = ((bf16[64,5,2,128]{3,2,1,0:T(2,128)(2,1)}), bf16[64,5,2,128]{3,2,1,0:T(2,128)(2,1)S(1)}, u32[]{:S(2)}, u32[]{:S(2)}) async-start(bf16[64,5,2,128]{3,2,1,0:T(2,128)(2,1)} %pack.1), calls=%async_computation | async-start | bytes 327680 | tf_op jit(solution)/shard_map/all_to_all | solution.py:30
  21.2 0.0 copy-start
  21.2 2.7 %private.1 = (bf16[4,16,128]{2,1,0:T(8,128)(2,1)}, bf16[4,16,128]{2,1,0:T(8,128)(2,1)}, f32[4,128]{1,0:T(4,128)}) custom-call(s32[1]{0:T(128)S(6)} %copy.11.refs_0_, s32[2,128]{1,0:T(2,128)} %bitcast.1, bf16[1,8192]{1,0:T(2,128)(2,1)} %refs_2_, bf16[1,128]{1,0:T(2,128)(2,1)} %refs_3_.1, bf16[1,128]{1,0:T(2,128)(2,1)} %refs_4_.1, ...), custom_call_target="tpu_custom_call" | custom-call | flops 8388608 | bytes 1048576 | tf_op jit(solution)/shard_map/private/pallas_call | solution.py:295
  23.9 0.0 copy-start.2
  23.9 0.0 copy-start.3
  23.9 2.1 %collective-permute-start = (bf16[4,16,128]{2,1,0:T(8,128)(2,1)}, bf16[4,16,128]{2,1,0:T(8,128)(2,1)S(1)}, u32[]{:S(2)}, u32[]{:S(2)}) collective-permute-start(bf16[4,16,128]{2,1,0:T(8,128)(2,1)} %get-tuple-element.17), channel_id=1, source_target_pairs={{0,1},{1,0},{2,3},{3,2},{4,5},{5,4},{6,7},{7,6},{8,9},{9,8},{10,11... | collective-permute-start | bytes 49160 | tf_op jit(solution)/shard_map/ppermute | solution.py:23
  25.9 0.0 copy-done
  26.0 0.2 turn.1.keys_ref
  26.2 1.1 %collective-permute-done.second_ref = bf16[4,16,128]{2,1,0:T(8,128)(2,1)S(1)} collective-permute-done((bf16[4,16,128]{2,1,0:T(8,128)(2,1)}, bf16[4,16,128]{2,1,0:T(8,128)(2,1)S(1)}, u32[]{:S(2)}, u32[]{:S(2)}) %collective-permute-start) | collective-permute-done | bytes 16416 | tf_op jit(solution)/shard_map/ppermute | solution.py:23
  27.3 5.9 %all-to-all-done.gathered_ref = bf16[64,5,2,128]{3,2,1,0:T(2,128)(2,1)S(1)} async-done(((bf16[64,5,2,128]{3,2,1,0:T(2,128)(2,1)}), bf16[64,5,2,128]{3,2,1,0:T(2,128)(2,1)S(1)}, u32[]{:S(2)}, u32[]{:S(2)}) %all-to-all-start) | async-done | bytes 163872 | tf_op jit(solution)/shard_map/all_to_all | solution.py:30
  33.2 0.0 copy-done.2
  33.2 0.0 copy-done.3
  33.2 2.0 %spans.1 = bf16[64,5,2,128]{3,2,1,0:T(2,128)(2,1)} custom-call(bf16[64,5,2,128]{3,2,1,0:T(2,128)(2,1)S(1)} %all-to-all-done.gathered_ref, f32[4,128]{1,0:T(4,128)S(1)} %copy-done.3, bf16[512,512]{1,0:T(8,128)(2,1)S(1)} %turn.1.keys_ref, bf16[4,512,128]{2,1,0:T(8,128)(2,1)S(1)} %copy-done.2), custom_call_target="tpu_custom_call" | custom-call | flops 536870912 | bytes 1572864 | tf_op jit(solution)/shard_map/spans/pallas_call | solution.py:318
  35.1 0.0 copy-start.1
  35.2 10.6 %all-to-all-start.1 = ((bf16[64,5,2,128]{3,2,1,0:T(2,128)(2,1)}), bf16[64,5,2,128]{3,2,1,0:T(2,128)(2,1)S(1)}, u32[]{:S(2)}, u32[]{:S(2)}) async-start(bf16[64,5,2,128]{3,2,1,0:T(2,128)(2,1)} %spans.1), calls=%async_computation.1 | async-start | bytes 327680 | tf_op jit(solution)/shard_map/all_to_all | solution.py:30
  45.8 0.0 copy-done.1
  45.8 0.1 fold.2
  45.9 2.8 %collective-permute-start.1 = (bf16[2,16,128]{2,1,0:T(8,128)(2,1)S(1)}, bf16[2,16,128]{2,1,0:T(8,128)(2,1)S(1)}, u32[]{:S(2)}, u32[]{:S(2)}) collective-permute-start(bf16[2,16,128]{2,1,0:T(8,128)(2,1)S(1)} %get-tuple-element.24), channel_id=1, source_target_pairs={{0,2},{1,3},{2,0},{3,1},{4,6},{5,7},{6,4},{7,5},{8,10},{9,11},{10,... | collective-permute-start | bytes 24584 | tf_op jit(solution)/shard_map/ppermute | solution.py:23
  48.6 2.8 %collective-permute-done.1.second_ref = bf16[2,16,128]{2,1,0:T(8,128)(2,1)S(1)} collective-permute-done((bf16[2,16,128]{2,1,0:T(8,128)(2,1)S(1)}, bf16[2,16,128]{2,1,0:T(8,128)(2,1)S(1)}, u32[]{:S(2)}, u32[]{:S(2)}) %collective-permute-start.1) | collective-permute-done | bytes 8224 | tf_op jit(solution)/shard_map/ppermute | solution.py:23
  51.4 0.1 fold.3
  51.5 2.4 %collective-permute-start.2 = (bf16[1,16,128]{2,1,0:T(8,128)(2,1)S(1)}, bf16[1,16,128]{2,1,0:T(8,128)(2,1)S(1)}, u32[]{:S(2)}, u32[]{:S(2)}) collective-permute-start(bf16[1,16,128]{2,1,0:T(8,128)(2,1)S(1)} %get-tuple-element.26), channel_id=1, source_target_pairs={{0,6},{1,7},{2,4},{3,5},{4,2},{5,3},{6,0},{7,1},{8,14},{9,15},{10,... | collective-permute-start | bytes 12296 | tf_op jit(solution)/shard_map/ppermute | solution.py:23
  53.9 4.3 %collective-permute-done.2.there_ref = bf16[1,16,128]{2,1,0:T(8,128)(2,1)S(1)} collective-permute-done((bf16[1,16,128]{2,1,0:T(8,128)(2,1)S(1)}, bf16[1,16,128]{2,1,0:T(8,128)(2,1)S(1)}, u32[]{:S(2)}, u32[]{:S(2)}) %collective-permute-start.2) | collective-permute-done | bytes 4128 | tf_op jit(solution)/shard_map/ppermute | solution.py:23
  58.2 0.0 all-to-all-done.1.spans_ref
  58.3 0.8 %merge.1 = bf16[1,1024]{1,0:T(2,128)(2,1)} custom-call(bf16[64,5,2,128]{3,2,1,0:T(2,128)(2,1)S(1)} %all-to-all-done.1.spans_ref, bf16[1,16,128]{2,1,0:T(8,128)(2,1)S(1)} %get-tuple-element.25.here_ref, bf16[1,16,128]{2,1,0:T(8,128)(2,1)S(1)} %collective-permute-done.2.there_ref), custom_call_target="tpu_custom_call" | custom-call | tf_op jit(solution)/shard_map/merge/pallas_call | solution.py:335
Async XLA Ops:
  1.4 31.8 %all-to-all-start = ((bf16[64,5,2,128]{3,2,1,0:T(2,128)(2,1)}), bf16[64,5,2,128]{3,2,1,0:T(2,128)(2,1)S(1)}, u32[]{:S(2)}, u32[]{:S(2)}) async-start(bf16[64,5,2,128]{3,2,1,0:T(2,128)(2,1)} %pack.1), calls=%async_computation | async-start | bytes 327680 | tf_op jit(solution)/shard_map/all_to_all | solution.py:30
  21.2 4.8 %copy-start = (bf16[4,512,128]{2,1,0:T(8,128)(2,1)S(1)}, bf16[4,512,128]{2,1,0:T(8,128)(2,1)}, u32[]{:S(2)}) copy-start(bf16[4,512,128]{2,1,0:T(8,128)(2,1)} %keys_ref) | copy-start | bytes 1572868
  23.9 9.3 %copy-start.2 = (bf16[4,512,128]{2,1,0:T(8,128)(2,1)S(1)}, bf16[4,512,128]{2,1,0:T(8,128)(2,1)}, u32[]{:S(2)}) copy-start(bf16[4,512,128]{2,1,0:T(8,128)(2,1)} %values_ref.1) | copy-start | bytes 1572868
  23.9 9.3 %copy-start.3 = (f32[4,128]{1,0:T(4,128)S(1)}, f32[4,128]{1,0:T(4,128)}, u32[]{:S(2)}) copy-start(f32[4,128]{1,0:T(4,128)} %get-tuple-element.19.idents_ref) | copy-start | bytes 6148
  23.9 3.4 %collective-permute-start = (bf16[4,16,128]{2,1,0:T(8,128)(2,1)}, bf16[4,16,128]{2,1,0:T(8,128)(2,1)S(1)}, u32[]{:S(2)}, u32[]{:S(2)}) collective-permute-start(bf16[4,16,128]{2,1,0:T(8,128)(2,1)} %get-tuple-element.17), channel_id=1, source_target_pairs={{0,1},{1,0},{2,3},{3,2},{4,5},{5,4},{6,7},{7,6},{8,9},{9,8},{10,11... | collective-permute-start | bytes 49160 | tf_op jit(solution)/shard_map/ppermute | solution.py:23
  35.1 10.6 %copy-start.1 = (bf16[4,16,128]{2,1,0:T(8,128)(2,1)S(1)}, bf16[4,16,128]{2,1,0:T(8,128)(2,1)}, u32[]{:S(2)}) copy-start(bf16[4,16,128]{2,1,0:T(8,128)(2,1)} %get-tuple-element.21.first_ref) | copy-start | bytes 49156
  35.2 23.1 %all-to-all-start.1 = ((bf16[64,5,2,128]{3,2,1,0:T(2,128)(2,1)}), bf16[64,5,2,128]{3,2,1,0:T(2,128)(2,1)S(1)}, u32[]{:S(2)}, u32[]{:S(2)}) async-start(bf16[64,5,2,128]{3,2,1,0:T(2,128)(2,1)} %spans.1), calls=%async_computation.1 | async-start | bytes 327680 | tf_op jit(solution)/shard_map/all_to_all | solution.py:30
  45.9 5.5 %collective-permute-start.1 = (bf16[2,16,128]{2,1,0:T(8,128)(2,1)S(1)}, bf16[2,16,128]{2,1,0:T(8,128)(2,1)S(1)}, u32[]{:S(2)}, u32[]{:S(2)}) collective-permute-start(bf16[2,16,128]{2,1,0:T(8,128)(2,1)S(1)} %get-tuple-element.24), channel_id=1, source_target_pairs={{0,2},{1,3},{2,0},{3,1},{4,6},{5,7},{6,4},{7,5},{8,10},{9,11},{10,... | collective-permute-start | bytes 24584 | tf_op jit(solution)/shard_map/ppermute | solution.py:23
  51.5 6.7 %collective-permute-start.2 = (bf16[1,16,128]{2,1,0:T(8,128)(2,1)S(1)}, bf16[1,16,128]{2,1,0:T(8,128)(2,1)S(1)}, u32[]{:S(2)}, u32[]{:S(2)}) collective-permute-start(bf16[1,16,128]{2,1,0:T(8,128)(2,1)S(1)} %get-tuple-element.26), channel_id=1, source_target_pairs={{0,6},{1,7},{2,4},{3,5},{4,2},{5,3},{6,0},{7,1},{8,14},{9,15},{10,... | collective-permute-start | bytes 12296 | tf_op jit(solution)/shard_map/ppermute | solution.py:23

commit v3 on v1

--- a/solution.py
+++ b/solution.py
@@ -11,6 +11,7 @@
 KVH = 8
 DH = 128
 CORES = 2
+ROWS = 10
 LOW = -1e30
 SCALE = 1.0 / DH**0.5
 F32 = jnp.float32
@@ -26,7 +27,9 @@
     n = lax.axis_size("span")
     first = n * 7 // 16
     order = [(first + k) % n for k in range(n)]
-    return lax.all_to_all(value, "span", 0, 0, axis_index_groups=[order], tiled=True)
+    blocks = value.reshape(n, ROWS // 2, 2, DH)
+    blocks = lax.all_to_all(blocks, "span", 0, 0, axis_index_groups=[order], tiled=True)
+    return blocks.reshape(value.shape)
 
 
 def split(lse):
@@ -48,19 +51,19 @@
     return result
 
 
-def diagonals(shape):
-    head = lax.broadcasted_iota(jnp.int32, shape, 1)
-    return [lanes(shape) == head + 8 * k for k in range(3)]
-
-
-def block_of(attended, lse):
-    count = attended.shape[0]
-    row = jnp.zeros(attended.shape, F32)
-    for where, part in zip(diagonals(attended.shape), split(lse)):
-        row = jnp.where(where, part, row)
-    row = jnp.sum(row, 1, keepdims=True)
-    row = jnp.broadcast_to(row, (count, 2, DH)).reshape(count, 1, 2, DH)
-    return jnp.concatenate([attended.reshape(count, 4, 2, DH), row], 1).astype(BF16)
+def diagonal(count):
+    shape = (count, 8, DH)
+    return lanes(shape) == lax.broadcasted_iota(jnp.int32, shape, 1)
+
+
+def heads_of(blocks, count):
+    return jnp.concatenate(
+        [blocks[k * ROWS : k * ROWS + 8] for k in range(count)], 0
+    ).reshape(count, 8, DH)
+
+
+def extras_of(blocks, count):
+    return jnp.concatenate([blocks[k * ROWS + 8 : k * ROWS + 9] for k in range(count)], 0)
 
 
 def fetch(pairs, sems):
@@ -80,10 +83,8 @@
     rows = [query[:, h * DH : (h + 1) * DH] for h in range(KVH)]
     ids = ids_ref[...].astype(F32)
     ids = jnp.concatenate([ids, jnp.full((1, DH - ids.shape[1]), -1.0, F32)], 1)
-    block = jnp.concatenate(rows + [ids, ids], 0).reshape(5, 2, DH).astype(BF16)
     count = held_ref.shape[0]
-    for copy in range(count):
-        held_ref[copy] = block
+    held_ref[...] = jnp.concatenate((rows + [ids, ids]) * (count // ROWS), 0).astype(BF16)
     places = range(0, out_ref.shape[0], count)
     pairs = [(held_ref, out_ref.at[pl.ds(place, count)]) for place in places]
     for copy in fetch(pairs, sems):
@@ -105,8 +106,8 @@
     chip = (mine - core) // CORES
     groups = [
         jnp.bitwise_xor(chip, step) * CORES + which
+        for step in (0, 3, 1, 2)
         for which in (core, 1 - core)
-        for step in (0, 3, 1, 2)
     ]
     heads = [pl.ds(pl.multiple_of(g * DH, DH), DH) for g in groups]
     scores = []
@@ -146,8 +147,8 @@
         if k == 0:
             numer = numer + own * value_ref[...].astype(F32)
         message = jnp.concatenate([numer / safe[rows], stats[rows]], 0).astype(BF16)
-        out_ref = here_ref if k < KVH // CORES else there_ref
-        out_ref[k % (KVH // CORES)] = message
+        out_ref = here_ref if k < KVH // 2 else there_ref
+        out_ref[k % (KVH // 2)] = message
     table = slots_ref[...]
     number = (
         lax.broadcasted_iota(jnp.int32, table.shape, 0) * table.shape[1]
@@ -162,23 +163,23 @@
     idents_ref[...] = jnp.concatenate(idents, 0).astype(F32)
 
 
-def span_kernel(gathered_ref, idents_ref, keys_ref, values_ref, out_ref):
+def span_kernel(gathered_ref, idents_ref, keys_ref, values_ref, out_ref, held_ref):
     columns = keys_ref.shape[0]
-    requests = gathered_ref.shape[0]
-    count = min(32, requests)
+    requests = gathered_ref.shape[0] // ROWS
+    count = requests // 2
     rows = count * 8
     keys = jnp.concatenate([keys_ref[column] for column in range(columns)], 1)
     values = jnp.concatenate([values_ref[column] for column in range(columns)], 1)
     for start in range(0, requests, count):
-        message = gathered_ref[start : start + count].astype(F32)
-        query = message[:, :4].reshape(rows, DH)
-        ids = message[:, 4, :1, :]
+        part = slice(start * ROWS, (start + count) * ROWS)
+        message = gathered_ref[part].astype(F32)
+        query = heads_of(message, count).reshape(rows, DH)
+        ids = extras_of(message, count)
         code = jnp.zeros_like(ids)
         for column in range(columns):
-            ident = idents_ref[column : column + 1, :][None]
-            code = jnp.where(ids == ident, column + 1.0, code)
+            code = jnp.where(ids == idents_ref[column : column + 1, :], column + 1.0, code)
         code = jnp.max(code, -1, keepdims=True)
-        code = jnp.broadcast_to(code, (count, 8, DH)).reshape(rows, DH)
+        code = jnp.broadcast_to(code[:, None, :], (count, 8, DH)).reshape(rows, DH)
         listed = [code == column + 1.0 for column in range(columns)]
         query = jnp.concatenate([jnp.where(here, query, 0.0) for here in listed], 1)
         score = SCALE * lax.dot_general(
@@ -192,8 +193,14 @@
         numer = jnp.zeros((rows, DH), F32)
         for column in range(columns):
             numer = jnp.where(listed[column], numers[:, column * DH : (column + 1) * DH], numer)
-        attended = (numer / total).reshape(count, 8, DH)
-        out_ref[start : start + count] = block_of(attended, lse.reshape(count, 8, 1))
+        attended = numer / total
+        lse = jnp.where(diagonal(count), lse.reshape(count, 8, 1), 0.0)
+        high, middle, last = split(jnp.sum(lse, 1))
+        extras = high + pltpu.roll(middle, 8, 1) + pltpu.roll(last, 16, 1)
+        for k in range(count):
+            held_ref[k * ROWS : k * ROWS + 8] = attended[k * 8 : k * 8 + 8]
+            held_ref[k * ROWS + 8 : k * ROWS + ROWS] = jnp.broadcast_to(extras[k : k + 1], (2, DH))
+        out_ref[part] = held_ref[...].astype(BF16)
 
 
 def fold_kernel(first_ref, second_ref, *out_refs):
@@ -211,21 +218,23 @@
 
 
 def merge_kernel(spans_ref, here_ref, there_ref, out_ref):
+    count = spans_ref.shape[0] // ROWS
     spans = spans_ref[...].astype(F32)
-    attended = spans[:, :4].reshape(-1, 8, DH)
-    row = jnp.broadcast_to(spans[:, 4, :1, :], attended.shape)
-    kept = functools.reduce(jnp.logical_or, diagonals(attended.shape))
-    lse = jnp.sum(jnp.where(kept, row, 0.0), -1, keepdims=True)
     tiles = [here_ref[0].astype(F32), there_ref[0].astype(F32)]
-    lses = [jnp.sum(tile[8:], -1, keepdims=True) for tile in tiles]
-    peak = functools.reduce(jnp.maximum, lses, jnp.max(lse, 0))
-    weight = jnp.exp(lse - peak[None])
-    weights = [jnp.exp(other - peak) for other in lses]
-    total = sum(weights, jnp.sum(weight, 0))
-    numer = sum(
-        (w * tile[:8] for w, tile in zip(weights, tiles)), jnp.sum(weight * attended, 0)
-    )
-    result = numer / total
+    attended = [tile[:8] for tile in tiles] + [heads_of(spans, count)]
+    parts = extras_of(spans, count)
+    lses = [
+        jnp.sum(jnp.where(diagonal(1)[0], jnp.sum(tile[8:], -1, keepdims=True), 0.0), 0)[None]
+        for tile in tiles
+    ] + [parts + pltpu.roll(parts, DH - 8, 1) + pltpu.roll(parts, DH - 16, 1)]
+    peak = functools.reduce(jnp.maximum, [jnp.max(lse, 0, keepdims=True) for lse in lses])
+    weights = [jnp.exp(lse - peak) for lse in lses]
+    scale = 1.0 / sum(jnp.sum(weight, 0, keepdims=True) for weight in weights)
+    result = jnp.zeros((8, DH), F32)
+    for weight, values in zip(weights, attended):
+        weight = (weight * scale)[:, None, :]
+        weight = jnp.sum(jnp.where(diagonal(weight.shape[0]), weight, 0.0), -1, keepdims=True)
+        result = result + jnp.sum(weight * values, 0)
     out_ref[...] = jnp.concatenate([result[h : h + 1] for h in range(8)], 1).astype(BF16)
 
 
@@ -250,11 +259,10 @@
     span_slots,
 ):
     requests = lax.axis_size("span")
-    chips = lax.axis_size("ctx") // CORES
     ch_dev = span_keys.shape[0]
     params = pltpu.CompilerParams(vmem_limit_bytes=16 * 1024 * 1024)
     alone = pltpu.CompilerParams(vmem_limit_bytes=56 * 1024 * 1024)
-    blocks = jax.ShapeDtypeStruct((requests, 5, 2, DH), BF16)
+    blocks = jax.ShapeDtypeStruct((requests * ROWS, DH), BF16)
 
     def tiles(count):
         return jax.ShapeDtypeStruct((count, 16, DH), BF16)
@@ -275,7 +283,7 @@
         in_specs=hbm(2),
         out_specs=hbm(1)[0],
         scratch_shapes=[
-            pltpu.VMEM((requests // 4,) + blocks.shape[1:], BF16),
+            pltpu.VMEM((blocks.shape[0] // 4, DH), BF16),
             pltpu.VMEM((1, KVH * DH), BF16),
             pltpu.VMEM(span_lists.shape, jnp.int32),
             pltpu.SemaphoreType.DMA((4,)),
@@ -289,9 +297,9 @@
     fetched = (table, queries, new_key, new_value, ctx_keys, ctx_values)
     here, there, idents = pl.pallas_call(
         private_kernel,
-        out_shape=[tiles(chips)] * CORES + [jax.ShapeDtypeStruct((ch_dev, DH), F32)],
+        out_shape=[tiles(KVH // 2)] * 2 + [jax.ShapeDtypeStruct((ch_dev, DH), F32)],
         in_specs=hbm(1 + len(fetched)),
-        out_specs=vmem(CORES + 1),
+        out_specs=vmem(3),
         scratch_shapes=[pltpu.SMEM(lengths.shape, jnp.int32)]
         + [pltpu.VMEM(array.shape, array.dtype) for array in fetched]
         + [pltpu.SemaphoreType.DMA((1 + len(fetched),))],
@@ -301,12 +309,13 @@
         ),
         name="private",
     )(lengths, *fetched)
-    there, gathered = lax.optimization_barrier((swapped(there, 1), gathered))
+    there, gathered = lax.optimization_barrier((swapped(there, CORES), gathered))
     partial = pl.pallas_call(
         span_kernel,
         out_shape=blocks,
         in_specs=vmem(4),
         out_specs=vmem(1)[0],
+        scratch_shapes=[pltpu.VMEM((blocks.shape[0] // 2, DH), F32)],
         compiler_params=params,
         cost_estimate=pl.CostEstimate(
             flops=4 * requests * 8 * DH * ch_dev * span_keys.shape[1],
@@ -316,9 +325,9 @@
         name="spans",
     )(gathered, idents, span_keys, span_values)
     partial = exchanged(partial)
-    for mask in (1, 3):
+    for mask in (3 * CORES, 1):
         here, there = fold(here, there)
-        there = swapped(there, mask * CORES)
+        there = swapped(there, mask)
     return pl.pallas_call(
         merge_kernel,
         out_shape=jax.ShapeDtypeStruct((1, KVH * DH), BF16),

time: 59.5 us -> 59.4 us (level)
  waiting for transfers between devices: 14.5 us -> 13.3 us
  starting transfers between devices: 36.8 us -> 37.9 us
    all_to_all x2, waiting for transfers between devices: 5.99 us -> 4.69 us  [exchanged(): lax.all_to_all(blocks, 'span', 0, 0, axis_index_groups=[order], tiled=True)]
    all_to_all x2, starting transfers between devices: 29.7 us -> 30.8 us  [exchanged(): lax.all_to_all(blocks, 'span', 0, 0, axis_index_groups=[order], tiled=True)]
  transfers between devices with their start and end apart: 5 -> 5, of which waited for: 4 -> 5; matrix products, arithmetic and copies ran while one was open for 0% -> 0% of each run, Pallas kernels for 5% -> 5%
where the time goes in v3:
time: 59.4 us; the launch traced here: 59 us
  starting transfers between devices  37.9 us (64%)
  waiting for transfers between devices  13.3 us (22%)
  Pallas kernels  7.1 us (12%)
  between operations  0.75 us (1%)
    all_to_all x2, starting transfers between devices, exchanged(): lax.all_to_all(blocks, 'span', 0, 0, axis_index_groups=[order], tiled=True)  30.8 us
    ppermute x3, waiting for transfers between devices, swapped(): return lax.ppermute(value, 'ctx', [(i, i ^ mask) for i in range(n)])  8.59 us
    ppermute x3, starting transfers between devices, swapped(): return lax.ppermute(value, 'ctx', [(i, i ^ mask) for i in range(n)])  7.04 us
    all_to_all x2, waiting for transfers between devices, exchanged(): lax.all_to_all(blocks, 'span', 0, 0, axis_index_groups=[order], tiled=True)  4.69 us
    pallas_call x1, Pallas kernels, shards(): pl.pallas_call(private_kernel, out_shape=[tiles(KVH // 2)] * 2 + [jax.Sha...  2.69 us
    pallas_call x1, Pallas kernels, shards(): pl.pallas_call(span_kernel, out_shape=blocks, in_specs=vmem(4), out_specs...  1.9 us
    pallas_call x1, Pallas kernels, shards(): pl.pallas_call(pack_kernel, out_shape=blocks, in_specs=hbm(2), out_specs=...  1.4 us
  transfers between devices with their start and end apart: 5, of which 5 were waited for; matrix products, arithmetic and copies ran while one was open for 0% of the time, Pallas kernels for 5%

profile of v3, /device:TPU:6, one launch (start us, length us, event | category | flops | bytes accessed | tf_op | source)
XLA Modules:
  0.0 59.0 jit_solution(3416057207099332981)
XLA Ops:
  0.0 1.4 %pack.1 = bf16[640,128]{1,0:T(8,128)(2,1)} custom-call(bf16[1,8192]{1,0:T(2,128)(2,1)} %refs_2_, s32[1,16]{1,0:T(1,128)} %lists_ref.1), custom_call_target="tpu_custom_call" | custom-call | tf_op jit(solution)/shard_map/pack/pallas_call | solution.py:280
  1.4 19.1 %all-to-all-start = ((bf16[64,5,2,128]{3,2,1,0:T(2,128)(2,1)}), bf16[64,5,2,128]{3,2,1,0:T(2,128)(2,1)S(1)}, u32[]{:S(2)}, u32[]{:S(2)}) async-start(bf16[64,5,2,128]{3,2,1,0:T(2,128)(2,1)} %bitcast.7), calls=%async_computation | async-start | bytes 327680 | tf_op jit(solution)/shard_map/all_to_all | solution.py:31
  21.2 0.0 copy-start.1
  21.2 0.0 copy-start.2
  21.2 2.7 %private.1 = (bf16[4,16,128]{2,1,0:T(8,128)(2,1)}, bf16[4,16,128]{2,1,0:T(8,128)(2,1)}, f32[4,128]{1,0:T(4,128)}) custom-call(s32[1]{0:T(128)S(6)} %copy.11.refs_0_, s32[2,128]{1,0:T(2,128)} %bitcast.8, bf16[1,8192]{1,0:T(2,128)(2,1)} %refs_2_, bf16[1,128]{1,0:T(2,128)(2,1)} %refs_3_.1, bf16[1,128]{1,0:T(2,128)(2,1)} %refs_4_.1, ...), custom_call_target="tpu_custom_call" | custom-call | flops 8388608 | bytes 1048576 | tf_op jit(solution)/shard_map/private/pallas_call | solution.py:298
  23.9 0.0 copy-start.3
  23.9 2.7 %collective-permute-start = (bf16[4,16,128]{2,1,0:T(8,128)(2,1)}, bf16[4,16,128]{2,1,0:T(8,128)(2,1)S(1)}, u32[]{:S(2)}, u32[]{:S(2)}) collective-permute-start(bf16[4,16,128]{2,1,0:T(8,128)(2,1)} %get-tuple-element.16), channel_id=1, source_target_pairs={{0,2},{1,3},{2,0},{3,1},{4,6},{5,7},{6,4},{7,5},{8,10},{9,11},{10,... | collective-permute-start | bytes 49160 | tf_op jit(solution)/shard_map/ppermute | solution.py:23
  26.6 3.1 %collective-permute-done.second_ref = bf16[4,16,128]{2,1,0:T(8,128)(2,1)S(1)} collective-permute-done((bf16[4,16,128]{2,1,0:T(8,128)(2,1)}, bf16[4,16,128]{2,1,0:T(8,128)(2,1)S(1)}, u32[]{:S(2)}, u32[]{:S(2)}) %collective-permute-start) | collective-permute-done | bytes 16416 | tf_op jit(solution)/shard_map/ppermute | solution.py:23
  29.7 3.4 %all-to-all-done = bf16[64,5,2,128]{3,2,1,0:T(2,128)(2,1)S(1)} async-done(((bf16[64,5,2,128]{3,2,1,0:T(2,128)(2,1)}), bf16[64,5,2,128]{3,2,1,0:T(2,128)(2,1)S(1)}, u32[]{:S(2)}, u32[]{:S(2)}) %all-to-all-start) | async-done | bytes 163872 | tf_op jit(solution)/shard_map/all_to_all | solution.py:31
  33.2 0.0 copy-done.1
  33.2 0.0 copy-done.2
  33.2 0.0 copy-done.3
  33.2 1.9 %spans.1 = bf16[640,128]{1,0:T(8,128)(2,1)} custom-call(bf16[640,128]{1,0:T(8,128)(2,1)S(1)} %bitcast.6, f32[4,128]{1,0:T(4,128)S(1)} %copy-done.3, bf16[4,512,128]{2,1,0:T(8,128)(2,1)S(1)} %copy-done.1, bf16[4,512,128]{2,1,0:T(8,128)(2,1)S(1)} %copy-done.2), custom_call_target="tpu_custom_call" | custom-call | flops 536870912 | bytes 1572864 | tf_op jit(solution)/shard_map/spans/pallas_call | solution.py:313
  35.1 0.0 copy-start
  35.1 11.7 %all-to-all-start.1 = ((bf16[64,5,2,128]{3,2,1,0:T(2,128)(2,1)}), bf16[64,5,2,128]{3,2,1,0:T(2,128)(2,1)S(1)}, u32[]{:S(2)}, u32[]{:S(2)}) async-start(bf16[64,5,2,128]{3,2,1,0:T(2,128)(2,1)} %bitcast.3), calls=%async_computation.1 | async-start | bytes 327680 | tf_op jit(solution)/shard_map/all_to_all | solution.py:31
  46.8 0.0 copy-done
  46.8 0.1 fold.2
  46.9 2.4 %collective-permute-start.1 = (bf16[2,16,128]{2,1,0:T(8,128)(2,1)S(1)}, bf16[2,16,128]{2,1,0:T(8,128)(2,1)S(1)}, u32[]{:S(2)}, u32[]{:S(2)}) collective-permute-start(bf16[2,16,128]{2,1,0:T(8,128)(2,1)S(1)} %get-tuple-element.22), channel_id=1, source_target_pairs={{0,6},{1,7},{2,4},{3,5},{4,2},{5,3},{6,0},{7,1},{8,14},{9,15},{10,... | collective-permute-start | bytes 24584 | tf_op jit(solution)/shard_map/ppermute | solution.py:23
  49.3 4.4 %collective-permute-done.1.second_ref = bf16[2,16,128]{2,1,0:T(8,128)(2,1)S(1)} collective-permute-done((bf16[2,16,128]{2,1,0:T(8,128)(2,1)S(1)}, bf16[2,16,128]{2,1,0:T(8,128)(2,1)S(1)}, u32[]{:S(2)}, u32[]{:S(2)}) %collective-permute-start.1) | collective-permute-done | bytes 8224 | tf_op jit(solution)/shard_map/ppermute | solution.py:23
  53.7 0.1 fold.3
  53.8 1.9 %collective-permute-start.2 = (bf16[1,16,128]{2,1,0:T(8,128)(2,1)S(1)}, bf16[1,16,128]{2,1,0:T(8,128)(2,1)S(1)}, u32[]{:S(2)}, u32[]{:S(2)}) collective-permute-start(bf16[1,16,128]{2,1,0:T(8,128)(2,1)S(1)} %get-tuple-element.24), channel_id=1, source_target_pairs={{0,1},{1,0},{2,3},{3,2},{4,5},{5,4},{6,7},{7,6},{8,9},{9,8},{10,11... | collective-permute-start | bytes 12296 | tf_op jit(solution)/shard_map/ppermute | solution.py:23
  55.7 1.1 %collective-permute-done.2.there_ref = bf16[1,16,128]{2,1,0:T(8,128)(2,1)S(1)} collective-permute-done((bf16[1,16,128]{2,1,0:T(8,128)(2,1)S(1)}, bf16[1,16,128]{2,1,0:T(8,128)(2,1)S(1)}, u32[]{:S(2)}, u32[]{:S(2)}) %collective-permute-start.2) | collective-permute-done | bytes 4128 | tf_op jit(solution)/shard_map/ppermute | solution.py:23
  56.9 1.3 %all-to-all-done.1 = bf16[64,5,2,128]{3,2,1,0:T(2,128)(2,1)S(1)} async-done(((bf16[64,5,2,128]{3,2,1,0:T(2,128)(2,1)}), bf16[64,5,2,128]{3,2,1,0:T(2,128)(2,1)S(1)}, u32[]{:S(2)}, u32[]{:S(2)}) %all-to-all-start.1) | async-done | bytes 163872 | tf_op jit(solution)/shard_map/all_to_all | solution.py:31
  58.1 0.9 %merge.1 = bf16[1,1024]{1,0:T(2,128)(2,1)} custom-call(bf16[640,128]{1,0:T(8,128)(2,1)S(1)} %bitcast.5, bf16[1,16,128]{2,1,0:T(8,128)(2,1)S(1)} %get-tuple-element.23.here_ref, bf16[1,16,128]{2,1,0:T(8,128)(2,1)S(1)} %collective-permute-done.2.there_ref), custom_call_target="tpu_custom_call" | custom-call | tf_op jit(solution)/shard_map/merge/pallas_call | solution.py:331
Async XLA Ops:
  1.4 31.8 %all-to-all-start = ((bf16[64,5,2,128]{3,2,1,0:T(2,128)(2,1)}), bf16[64,5,2,128]{3,2,1,0:T(2,128)(2,1)S(1)}, u32[]{:S(2)}, u32[]{:S(2)}) async-start(bf16[64,5,2,128]{3,2,1,0:T(2,128)(2,1)} %bitcast.7), calls=%async_computation | async-start | bytes 327680 | tf_op jit(solution)/shard_map/all_to_all | solution.py:31
  21.2 12.0 %copy-start.1 = (bf16[4,512,128]{2,1,0:T(8,128)(2,1)S(1)}, bf16[4,512,128]{2,1,0:T(8,128)(2,1)}, u32[]{:S(2)}) copy-start(bf16[4,512,128]{2,1,0:T(8,128)(2,1)} %keys_ref.1) | copy-start | bytes 1572868
  21.2 12.0 %copy-start.2 = (bf16[4,512,128]{2,1,0:T(8,128)(2,1)S(1)}, bf16[4,512,128]{2,1,0:T(8,128)(2,1)}, u32[]{:S(2)}) copy-start(bf16[4,512,128]{2,1,0:T(8,128)(2,1)} %values_ref.1) | copy-start | bytes 1572868
  23.9 9.3 %copy-start.3 = (f32[4,128]{1,0:T(4,128)S(1)}, f32[4,128]{1,0:T(4,128)}, u32[]{:S(2)}) copy-start(f32[4,128]{1,0:T(4,128)} %get-tuple-element.18.idents_ref) | copy-start | bytes 6148
  23.9 5.8 %collective-permute-start = (bf16[4,16,128]{2,1,0:T(8,128)(2,1)}, bf16[4,16,128]{2,1,0:T(8,128)(2,1)S(1)}, u32[]{:S(2)}, u32[]{:S(2)}) collective-permute-start(bf16[4,16,128]{2,1,0:T(8,128)(2,1)} %get-tuple-element.16), channel_id=1, source_target_pairs={{0,2},{1,3},{2,0},{3,1},{4,6},{5,7},{6,4},{7,5},{8,10},{9,11},{10,... | collective-permute-start | bytes 49160 | tf_op jit(solution)/shard_map/ppermute | solution.py:23
  35.1 11.7 %copy-start = (bf16[4,16,128]{2,1,0:T(8,128)(2,1)S(1)}, bf16[4,16,128]{2,1,0:T(8,128)(2,1)}, u32[]{:S(2)}) copy-start(bf16[4,16,128]{2,1,0:T(8,128)(2,1)} %get-tuple-element.19.first_ref) | copy-start | bytes 49156
  35.1 23.0 %all-to-all-start.1 = ((bf16[64,5,2,128]{3,2,1,0:T(2,128)(2,1)}), bf16[64,5,2,128]{3,2,1,0:T(2,128)(2,1)S(1)}, u32[]{:S(2)}, u32[]{:S(2)}) async-start(bf16[64,5,2,128]{3,2,1,0:T(2,128)(2,1)} %bitcast.3), calls=%async_computation.1 | async-start | bytes 327680 | tf_op jit(solution)/shard_map/all_to_all | solution.py:31
  46.9 6.8 %collective-permute-start.1 = (bf16[2,16,128]{2,1,0:T(8,128)(2,1)S(1)}, bf16[2,16,128]{2,1,0:T(8,128)(2,1)S(1)}, u32[]{:S(2)}, u32[]{:S(2)}) collective-permute-start(bf16[2,16,128]{2,1,0:T(8,128)(2,1)S(1)} %get-tuple-element.22), channel_id=1, source_target_pairs={{0,6},{1,7},{2,4},{3,5},{4,2},{5,3},{6,0},{7,1},{8,14},{9,15},{10,... | collective-permute-start | bytes 24584 | tf_op jit(solution)/shard_map/ppermute | solution.py:23
  53.8 3.1 %collective-permute-start.2 = (bf16[1,16,128]{2,1,0:T(8,128)(2,1)S(1)}, bf16[1,16,128]{2,1,0:T(8,128)(2,1)S(1)}, u32[]{:S(2)}, u32[]{:S(2)}) collective-permute-start(bf16[1,16,128]{2,1,0:T(8,128)(2,1)S(1)} %get-tuple-element.24), channel_id=1, source_target_pairs={{0,1},{1,0},{2,3},{3,2},{4,5},{5,4},{6,7},{7,6},{8,9},{9,8},{10,11... | collective-permute-start | bytes 12296 | tf_op jit(solution)/shard_map/ppermute | solution.py:23

commit v4 on v3

--- a/solution.py
+++ b/solution.py
@@ -23,9 +23,13 @@
     return lax.ppermute(value, "ctx", [(i, i ^ mask) for i in range(n)])
 
 
-def exchanged(value):
+def firsts():
     n = lax.axis_size("span")
-    first = n * 7 // 16
+    return n * 7 // 16, n * 29 // 64
+
+
+def exchanged(value, first):
+    n = lax.axis_size("span")
     order = [(first + k) % n for k in range(n)]
     blocks = value.reshape(n, ROWS // 2, 2, DH)
     blocks = lax.all_to_all(blocks, "span", 0, 0, axis_index_groups=[order], tiled=True)
@@ -106,8 +110,8 @@
     chip = (mine - core) // CORES
     groups = [
         jnp.bitwise_xor(chip, step) * CORES + which
+        for which in (core, 1 - core)
         for step in (0, 3, 1, 2)
-        for which in (core, 1 - core)
     ]
     heads = [pl.ds(pl.multiple_of(g * DH, DH), DH) for g in groups]
     scores = []
@@ -147,8 +151,8 @@
         if k == 0:
             numer = numer + own * value_ref[...].astype(F32)
         message = jnp.concatenate([numer / safe[rows], stats[rows]], 0).astype(BF16)
-        out_ref = here_ref if k < KVH // 2 else there_ref
-        out_ref[k % (KVH // 2)] = message
+        out_ref = here_ref if k < KVH // CORES else there_ref
+        out_ref[k % (KVH // CORES)] = message
     table = slots_ref[...]
     number = (
         lax.broadcasted_iota(jnp.int32, table.shape, 0) * table.shape[1]
@@ -167,6 +171,7 @@
     columns = keys_ref.shape[0]
     requests = gathered_ref.shape[0] // ROWS
     count = requests // 2
+    there, back = firsts()
     rows = count * 8
     keys = jnp.concatenate([keys_ref[column] for column in range(columns)], 1)
     values = jnp.concatenate([values_ref[column] for column in range(columns)], 1)
@@ -198,9 +203,10 @@
         high, middle, last = split(jnp.sum(lse, 1))
         extras = high + pltpu.roll(middle, 8, 1) + pltpu.roll(last, 16, 1)
         for k in range(count):
-            held_ref[k * ROWS : k * ROWS + 8] = attended[k * 8 : k * 8 + 8]
-            held_ref[k * ROWS + 8 : k * ROWS + ROWS] = jnp.broadcast_to(extras[k : k + 1], (2, DH))
-        out_ref[part] = held_ref[...].astype(BF16)
+            row = (start + k + there - back) % requests * ROWS
+            held_ref[row : row + 8] = attended[k * 8 : k * 8 + 8]
+            held_ref[row + 8 : row + ROWS] = jnp.broadcast_to(extras[k : k + 1], (2, DH))
+    out_ref[...] = held_ref[...].astype(BF16)
 
 
 def fold_kernel(first_ref, second_ref, *out_refs):
@@ -259,6 +265,7 @@
     span_slots,
 ):
     requests = lax.axis_size("span")
+    chips = lax.axis_size("ctx") // CORES
     ch_dev = span_keys.shape[0]
     params = pltpu.CompilerParams(vmem_limit_bytes=16 * 1024 * 1024)
     alone = pltpu.CompilerParams(vmem_limit_bytes=56 * 1024 * 1024)
@@ -291,15 +298,15 @@
         compiler_params=alone,
         name="pack",
     )(queries, span_lists)
-    gathered = exchanged(packed)
+    gathered = exchanged(packed, firsts()[0])
     queries, packed = lax.optimization_barrier((queries, packed))
     table = span_slots.reshape(-1, min(DH, span_slots.shape[0]))
     fetched = (table, queries, new_key, new_value, ctx_keys, ctx_values)
     here, there, idents = pl.pallas_call(
         private_kernel,
-        out_shape=[tiles(KVH // 2)] * 2 + [jax.ShapeDtypeStruct((ch_dev, DH), F32)],
+        out_shape=[tiles(chips)] * CORES + [jax.ShapeDtypeStruct((ch_dev, DH), F32)],
         in_specs=hbm(1 + len(fetched)),
-        out_specs=vmem(3),
+        out_specs=vmem(CORES + 1),
         scratch_shapes=[pltpu.SMEM(lengths.shape, jnp.int32)]
         + [pltpu.VMEM(array.shape, array.dtype) for array in fetched]
         + [pltpu.SemaphoreType.DMA((1 + len(fetched),))],
@@ -309,13 +316,13 @@
         ),
         name="private",
     )(lengths, *fetched)
-    there, gathered = lax.optimization_barrier((swapped(there, CORES), gathered))
+    there, gathered = lax.optimization_barrier((swapped(there, 1), gathered))
     partial = pl.pallas_call(
         span_kernel,
         out_shape=blocks,
         in_specs=vmem(4),
         out_specs=vmem(1)[0],
-        scratch_shapes=[pltpu.VMEM((blocks.shape[0] // 2, DH), F32)],
+        scratch_shapes=[pltpu.VMEM(blocks.shape, F32)],
         compiler_params=params,
         cost_estimate=pl.CostEstimate(
             flops=4 * requests * 8 * DH * ch_dev * span_keys.shape[1],
@@ -324,10 +331,10 @@
         ),
         name="spans",
     )(gathered, idents, span_keys, span_values)
-    partial = exchanged(partial)
-    for mask in (3 * CORES, 1):
+    partial = exchanged(partial, firsts()[1])
+    for mask in (1, 3):
         here, there = fold(here, there)
-        there = swapped(there, mask)
+        there = swapped(there, mask * CORES)
     return pl.pallas_call(
         merge_kernel,
         out_shape=jax.ShapeDtypeStruct((1, KVH * DH), BF16),

time: 59.4 us -> 59.5 us (level)
  waiting for transfers between devices: 13.3 us -> 14.5 us
  starting transfers between devices: 37.9 us -> 36.8 us
    all_to_all x2, waiting for transfers between devices: 4.69 us -> 5.99 us  [exchanged(): lax.all_to_all(blocks, 'span', 0, 0, axis_index_groups=[order], tiled=True)]
    all_to_all x2, starting transfers between devices: 30.8 us -> 29.7 us  [exchanged(): lax.all_to_all(blocks, 'span', 0, 0, axis_index_groups=[order], tiled=True)]
  transfers between devices with their start and end apart: 5 -> 5, of which waited for: 5 -> 4; matrix products, arithmetic and copies ran while one was open for 0% -> 0% of each run, Pallas kernels for 5% -> 5%
where the time goes in v4:
time: 59.5 us; the launch traced here: 59.1 us
  starting transfers between devices  36.8 us (62%)
  waiting for transfers between devices  14.5 us (24%)
  Pallas kernels  7.1 us (12%)
  between operations  0.75 us (1%)
    all_to_all x2, starting transfers between devices, exchanged(): lax.all_to_all(blocks, 'span', 0, 0, axis_index_groups=[order], tiled=True)  29.7 us
    ppermute x3, waiting for transfers between devices, swapped(): return lax.ppermute(value, 'ctx', [(i, i ^ mask) for i in range(n)])  8.46 us
    ppermute x3, starting transfers between devices, swapped(): return lax.ppermute(value, 'ctx', [(i, i ^ mask) for i in range(n)])  7.06 us
    all_to_all x2, waiting for transfers between devices, exchanged(): lax.all_to_all(blocks, 'span', 0, 0, axis_index_groups=[order], tiled=True)  5.99 us
    pallas_call x1, Pallas kernels, shards(): pl.pallas_call(private_kernel, out_shape=[tiles(chips)] * CORES + [jax.Sh...  2.69 us
    pallas_call x1, Pallas kernels, shards(): pl.pallas_call(span_kernel, out_shape=blocks, in_specs=vmem(4), out_specs...  1.91 us
    pallas_call x1, Pallas kernels, shards(): pl.pallas_call(pack_kernel, out_shape=blocks, in_specs=hbm(2), out_specs=...  1.4 us
  transfers between devices with their start and end apart: 5, of which 4 were waited for; matrix products, arithmetic and copies ran while one was open for 0% of the time, Pallas kernels for 5%

profile of v4, /device:TPU:6, one launch (start us, length us, event | category | flops | bytes accessed | tf_op | source)
XLA Modules:
  0.0 59.1 jit_solution(2088773843273093371)
XLA Ops:
  0.0 1.4 %pack.1 = bf16[640,128]{1,0:T(8,128)(2,1)} custom-call(bf16[1,8192]{1,0:T(2,128)(2,1)} %refs_2_, s32[1,16]{1,0:T(1,128)} %lists_ref.1), custom_call_target="tpu_custom_call" | custom-call | tf_op jit(solution)/shard_map/pack/pallas_call | solution.py:287
  1.4 19.1 %all-to-all-start = ((bf16[64,5,2,128]{3,2,1,0:T(2,128)(2,1)}), bf16[64,5,2,128]{3,2,1,0:T(2,128)(2,1)S(1)}, u32[]{:S(2)}, u32[]{:S(2)}) async-start(bf16[64,5,2,128]{3,2,1,0:T(2,128)(2,1)} %bitcast.7), calls=%async_computation | async-start | bytes 327680 | tf_op jit(solution)/shard_map/all_to_all | solution.py:35
  21.2 0.0 copy-start.1
  21.2 0.0 copy-start.2
  21.2 2.7 %private.1 = (bf16[4,16,128]{2,1,0:T(8,128)(2,1)}, bf16[4,16,128]{2,1,0:T(8,128)(2,1)}, f32[4,128]{1,0:T(4,128)}) custom-call(s32[1]{0:T(128)S(6)} %copy.11.refs_0_, s32[2,128]{1,0:T(2,128)} %bitcast.8, bf16[1,8192]{1,0:T(2,128)(2,1)} %refs_2_, bf16[1,128]{1,0:T(2,128)(2,1)} %refs_3_.1, bf16[1,128]{1,0:T(2,128)(2,1)} %refs_4_.1, ...), custom_call_target="tpu_custom_call" | custom-call | flops 8388608 | bytes 1048576 | tf_op jit(solution)/shard_map/private/pallas_call | solution.py:305
  23.9 0.0 copy-start.3
  23.9 1.9 %collective-permute-start = (bf16[4,16,128]{2,1,0:T(8,128)(2,1)}, bf16[4,16,128]{2,1,0:T(8,128)(2,1)S(1)}, u32[]{:S(2)}, u32[]{:S(2)}) collective-permute-start(bf16[4,16,128]{2,1,0:T(8,128)(2,1)} %get-tuple-element.16), channel_id=1, source_target_pairs={{0,1},{1,0},{2,3},{3,2},{4,5},{5,4},{6,7},{7,6},{8,9},{9,8},{10,11... | collective-permute-start | bytes 49160 | tf_op jit(solution)/shard_map/ppermute | solution.py:23
  25.8 1.4 %collective-permute-done.second_ref = bf16[4,16,128]{2,1,0:T(8,128)(2,1)S(1)} collective-permute-done((bf16[4,16,128]{2,1,0:T(8,128)(2,1)}, bf16[4,16,128]{2,1,0:T(8,128)(2,1)S(1)}, u32[]{:S(2)}, u32[]{:S(2)}) %collective-permute-start) | collective-permute-done | bytes 16416 | tf_op jit(solution)/shard_map/ppermute | solution.py:23
  27.2 6.0 %all-to-all-done = bf16[64,5,2,128]{3,2,1,0:T(2,128)(2,1)S(1)} async-done(((bf16[64,5,2,128]{3,2,1,0:T(2,128)(2,1)}), bf16[64,5,2,128]{3,2,1,0:T(2,128)(2,1)S(1)}, u32[]{:S(2)}, u32[]{:S(2)}) %all-to-all-start) | async-done | bytes 163872 | tf_op jit(solution)/shard_map/all_to_all | solution.py:35
  33.2 0.0 copy-done.1
  33.2 0.0 copy-done.2
  33.2 0.0 copy-done.3
  33.2 1.9 %spans.1 = bf16[640,128]{1,0:T(8,128)(2,1)} custom-call(bf16[640,128]{1,0:T(8,128)(2,1)S(1)} %bitcast.6, f32[4,128]{1,0:T(4,128)S(1)} %copy-done.3, bf16[4,512,128]{2,1,0:T(8,128)(2,1)S(1)} %copy-done.1, bf16[4,512,128]{2,1,0:T(8,128)(2,1)S(1)} %copy-done.2), custom_call_target="tpu_custom_call" | custom-call | flops 536870912 | bytes 1572864 | tf_op jit(solution)/shard_map/spans/pallas_call | solution.py:320
  35.1 0.0 copy-start
  35.1 10.6 %all-to-all-start.1 = ((bf16[64,5,2,128]{3,2,1,0:T(2,128)(2,1)}), bf16[64,5,2,128]{3,2,1,0:T(2,128)(2,1)S(1)}, u32[]{:S(2)}, u32[]{:S(2)}) async-start(bf16[64,5,2,128]{3,2,1,0:T(2,128)(2,1)} %bitcast.3), calls=%async_computation.1 | async-start | bytes 327680 | tf_op jit(solution)/shard_map/all_to_all | solution.py:35
  45.7 0.0 copy-done
  45.7 0.1 fold.2
  45.8 2.7 %collective-permute-start.1 = (bf16[2,16,128]{2,1,0:T(8,128)(2,1)S(1)}, bf16[2,16,128]{2,1,0:T(8,128)(2,1)S(1)}, u32[]{:S(2)}, u32[]{:S(2)}) collective-permute-start(bf16[2,16,128]{2,1,0:T(8,128)(2,1)S(1)} %get-tuple-element.22), channel_id=1, source_target_pairs={{0,2},{1,3},{2,0},{3,1},{4,6},{5,7},{6,4},{7,5},{8,10},{9,11},{10,... | collective-permute-start | bytes 24584 | tf_op jit(solution)/shard_map/ppermute | solution.py:23
  48.6 2.8 %collective-permute-done.1.second_ref = bf16[2,16,128]{2,1,0:T(8,128)(2,1)S(1)} collective-permute-done((bf16[2,16,128]{2,1,0:T(8,128)(2,1)S(1)}, bf16[2,16,128]{2,1,0:T(8,128)(2,1)S(1)}, u32[]{:S(2)}, u32[]{:S(2)}) %collective-permute-start.1) | collective-permute-done | bytes 8224 | tf_op jit(solution)/shard_map/ppermute | solution.py:23
  51.4 0.1 fold.3
  51.5 2.4 %collective-permute-start.2 = (bf16[1,16,128]{2,1,0:T(8,128)(2,1)S(1)}, bf16[1,16,128]{2,1,0:T(8,128)(2,1)S(1)}, u32[]{:S(2)}, u32[]{:S(2)}) collective-permute-start(bf16[1,16,128]{2,1,0:T(8,128)(2,1)S(1)} %get-tuple-element.24), channel_id=1, source_target_pairs={{0,6},{1,7},{2,4},{3,5},{4,2},{5,3},{6,0},{7,1},{8,14},{9,15},{10,... | collective-permute-start | bytes 12296 | tf_op jit(solution)/shard_map/ppermute | solution.py:23
  53.9 4.3 %collective-permute-done.2.there_ref = bf16[1,16,128]{2,1,0:T(8,128)(2,1)S(1)} collective-permute-done((bf16[1,16,128]{2,1,0:T(8,128)(2,1)S(1)}, bf16[1,16,128]{2,1,0:T(8,128)(2,1)S(1)}, u32[]{:S(2)}, u32[]{:S(2)}) %collective-permute-start.2) | collective-permute-done | bytes 4128 | tf_op jit(solution)/shard_map/ppermute | solution.py:23
  58.2 0.0 all-to-all-done.1
  58.2 0.9 %merge.1 = bf16[1,1024]{1,0:T(2,128)(2,1)} custom-call(bf16[640,128]{1,0:T(8,128)(2,1)S(1)} %bitcast.5, bf16[1,16,128]{2,1,0:T(8,128)(2,1)S(1)} %get-tuple-element.23.here_ref, bf16[1,16,128]{2,1,0:T(8,128)(2,1)S(1)} %collective-permute-done.2.there_ref), custom_call_target="tpu_custom_call" | custom-call | tf_op jit(solution)/shard_map/merge/pallas_call | solution.py:338
Async XLA Ops:
  1.4 31.8 %all-to-all-start = ((bf16[64,5,2,128]{3,2,1,0:T(2,128)(2,1)}), bf16[64,5,2,128]{3,2,1,0:T(2,128)(2,1)S(1)}, u32[]{:S(2)}, u32[]{:S(2)}) async-start(bf16[64,5,2,128]{3,2,1,0:T(2,128)(2,1)} %bitcast.7), calls=%async_computation | async-start | bytes 327680 | tf_op jit(solution)/shard_map/all_to_all | solution.py:35
  21.2 12.0 %copy-start.1 = (bf16[4,512,128]{2,1,0:T(8,128)(2,1)S(1)}, bf16[4,512,128]{2,1,0:T(8,128)(2,1)}, u32[]{:S(2)}) copy-start(bf16[4,512,128]{2,1,0:T(8,128)(2,1)} %keys_ref.1) | copy-start | bytes 1572868
  21.2 12.0 %copy-start.2 = (bf16[4,512,128]{2,1,0:T(8,128)(2,1)S(1)}, bf16[4,512,128]{2,1,0:T(8,128)(2,1)}, u32[]{:S(2)}) copy-start(bf16[4,512,128]{2,1,0:T(8,128)(2,1)} %values_ref.1) | copy-start | bytes 1572868
  23.9 9.3 %copy-start.3 = (f32[4,128]{1,0:T(4,128)S(1)}, f32[4,128]{1,0:T(4,128)}, u32[]{:S(2)}) copy-start(f32[4,128]{1,0:T(4,128)} %get-tuple-element.18.idents_ref) | copy-start | bytes 6148
  23.9 3.3 %collective-permute-start = (bf16[4,16,128]{2,1,0:T(8,128)(2,1)}, bf16[4,16,128]{2,1,0:T(8,128)(2,1)S(1)}, u32[]{:S(2)}, u32[]{:S(2)}) collective-permute-start(bf16[4,16,128]{2,1,0:T(8,128)(2,1)} %get-tuple-element.16), channel_id=1, source_target_pairs={{0,1},{1,0},{2,3},{3,2},{4,5},{5,4},{6,7},{7,6},{8,9},{9,8},{10,11... | collective-permute-start | bytes 49160 | tf_op jit(solution)/shard_map/ppermute | solution.py:23
  35.1 10.6 %copy-start = (bf16[4,16,128]{2,1,0:T(8,128)(2,1)S(1)}, bf16[4,16,128]{2,1,0:T(8,128)(2,1)}, u32[]{:S(2)}) copy-start(bf16[4,16,128]{2,1,0:T(8,128)(2,1)} %get-tuple-element.19.first_ref) | copy-start | bytes 49156
  35.1 23.1 %all-to-all-start.1 = ((bf16[64,5,2,128]{3,2,1,0:T(2,128)(2,1)}), bf16[64,5,2,128]{3,2,1,0:T(2,128)(2,1)S(1)}, u32[]{:S(2)}, u32[]{:S(2)}) async-start(bf16[64,5,2,128]{3,2,1,0:T(2,128)(2,1)} %bitcast.3), calls=%async_computation.1 | async-start | bytes 327680 | tf_op jit(solution)/shard_map/all_to_all | solution.py:35
  45.8 5.5 %collective-permute-start.1 = (bf16[2,16,128]{2,1,0:T(8,128)(2,1)S(1)}, bf16[2,16,128]{2,1,0:T(8,128)(2,1)S(1)}, u32[]{:S(2)}, u32[]{:S(2)}) collective-permute-start(bf16[2,16,128]{2,1,0:T(8,128)(2,1)S(1)} %get-tuple-element.22), channel_id=1, source_target_pairs={{0,2},{1,3},{2,0},{3,1},{4,6},{5,7},{6,4},{7,5},{8,10},{9,11},{10,... | collective-permute-start | bytes 24584 | tf_op jit(solution)/shard_map/ppermute | solution.py:23
  51.5 6.7 %collective-permute-start.2 = (bf16[1,16,128]{2,1,0:T(8,128)(2,1)S(1)}, bf16[1,16,128]{2,1,0:T(8,128)(2,1)S(1)}, u32[]{:S(2)}, u32[]{:S(2)}) collective-permute-start(bf16[1,16,128]{2,1,0:T(8,128)(2,1)S(1)} %get-tuple-element.24), channel_id=1, source_target_pairs={{0,6},{1,7},{2,4},{3,5},{4,2},{5,3},{6,0},{7,1},{8,14},{9,15},{10,... | collective-permute-start | bytes 12296 | tf_op jit(solution)/shard_map/ppermute | solution.py:23

commit v5 on v2

--- a/solution.py
+++ b/solution.py
@@ -25,7 +25,7 @@
 
 def exchanged(value):
     n = lax.axis_size("span")
-    first = n * 7 // 16
+    first = n * 29 // 64
     order = [(first + k) % n for k in range(n)]
     return lax.all_to_all(value, "span", 0, 0, axis_index_groups=[order], tiled=True)
 

time: 59.5 us -> 59.5 us (level)
  waiting for transfers between devices: 14.1 us -> 14.8 us
  starting transfers between devices: 36.9 us -> 36.2 us
    all_to_all x2, starting transfers between devices: 29.7 us -> 29 us  [exchanged(): lax.all_to_all(value, 'span', 0, 0, axis_index_groups=[order], tiled=True)]
    all_to_all x2, waiting for transfers between devices: 5.89 us -> 6.56 us  [exchanged(): lax.all_to_all(value, 'span', 0, 0, axis_index_groups=[order], tiled=True)]
where the time goes in v5:
time: 59.5 us; the launch traced here: 59.1 us
  starting transfers between devices  36.2 us (61%)
  waiting for transfers between devices  14.8 us (25%)
  Pallas kernels  7.29 us (12%)
  between operations  0.77 us (1%)
    all_to_all x2, starting transfers between devices, exchanged(): lax.all_to_all(value, 'span', 0, 0, axis_index_groups=[order], tiled=True)  29 us
    ppermute x3, waiting for transfers between devices, swapped(): return lax.ppermute(value, 'ctx', [(i, i ^ mask) for i in range(n)])  8.26 us
    ppermute x3, starting transfers between devices, swapped(): return lax.ppermute(value, 'ctx', [(i, i ^ mask) for i in range(n)])  7.17 us
    all_to_all x2, waiting for transfers between devices, exchanged(): lax.all_to_all(value, 'span', 0, 0, axis_index_groups=[order], tiled=True)  6.56 us
    pallas_call x1, Pallas kernels, shards(): pl.pallas_call(private_kernel, out_shape=[tiles(chips)] * CORES + [jax.Sh...  2.67 us
    pallas_call x1, Pallas kernels, shards(): pl.pallas_call(span_kernel, out_shape=blocks, in_specs=vmem(4), out_specs...  1.95 us
    pallas_call x1, Pallas kernels, shards(): pl.pallas_call(pack_kernel, out_shape=blocks, in_specs=hbm(2), out_specs=...  1.42 us
  transfers between devices with their start and end apart: 5, of which 4 were waited for; matrix products, arithmetic and copies ran while one was open for 0% of the time, Pallas kernels for 5%

profile of v5, /device:TPU:6, one launch (start us, length us, event | category | flops | bytes accessed | tf_op | source)
XLA Modules:
  0.0 59.1 jit_solution(595602023484468666)
XLA Ops:
  0.0 1.4 %pack.1 = bf16[64,5,2,128]{3,2,1,0:T(2,128)(2,1)} custom-call(bf16[1,8192]{1,0:T(2,128)(2,1)} %refs_2_, s32[1,16]{1,0:T(1,128)} %lists_ref.1), custom_call_target="tpu_custom_call" | custom-call | tf_op jit(solution)/shard_map/pack/pallas_call | solution.py:277
  1.4 19.1 %all-to-all-start = ((bf16[64,5,2,128]{3,2,1,0:T(2,128)(2,1)}), bf16[64,5,2,128]{3,2,1,0:T(2,128)(2,1)S(1)}, u32[]{:S(2)}, u32[]{:S(2)}) async-start(bf16[64,5,2,128]{3,2,1,0:T(2,128)(2,1)} %pack.1), calls=%async_computation | async-start | bytes 327680 | tf_op jit(solution)/shard_map/all_to_all | solution.py:30
  21.2 0.0 copy-start
  21.2 2.7 %private.1 = (bf16[4,16,128]{2,1,0:T(8,128)(2,1)}, bf16[4,16,128]{2,1,0:T(8,128)(2,1)}, f32[4,128]{1,0:T(4,128)}) custom-call(s32[1]{0:T(128)S(6)} %copy.11.refs_0_, s32[2,128]{1,0:T(2,128)} %bitcast.1, bf16[1,8192]{1,0:T(2,128)(2,1)} %refs_2_, bf16[1,128]{1,0:T(2,128)(2,1)} %refs_3_.1, bf16[1,128]{1,0:T(2,128)(2,1)} %refs_4_.1, ...), custom_call_target="tpu_custom_call" | custom-call | flops 8388608 | bytes 1048576 | tf_op jit(solution)/shard_map/private/pallas_call | solution.py:295
  23.9 0.0 copy-start.2
  23.9 0.0 copy-start.3
  23.9 2.1 %collective-permute-start = (bf16[4,16,128]{2,1,0:T(8,128)(2,1)}, bf16[4,16,128]{2,1,0:T(8,128)(2,1)S(1)}, u32[]{:S(2)}, u32[]{:S(2)}) collective-permute-start(bf16[4,16,128]{2,1,0:T(8,128)(2,1)} %get-tuple-element.17), channel_id=1, source_target_pairs={{0,1},{1,0},{2,3},{3,2},{4,5},{5,4},{6,7},{7,6},{8,9},{9,8},{10,11... | collective-permute-start | bytes 49160 | tf_op jit(solution)/shard_map/ppermute | solution.py:23
  25.9 0.0 copy-done
  25.9 0.2 turn.1.keys_ref
  26.2 1.1 %collective-permute-done.second_ref = bf16[4,16,128]{2,1,0:T(8,128)(2,1)S(1)} collective-permute-done((bf16[4,16,128]{2,1,0:T(8,128)(2,1)}, bf16[4,16,128]{2,1,0:T(8,128)(2,1)S(1)}, u32[]{:S(2)}, u32[]{:S(2)}) %collective-permute-start) | collective-permute-done | bytes 16416 | tf_op jit(solution)/shard_map/ppermute | solution.py:23
  27.3 6.6 %all-to-all-done.gathered_ref = bf16[64,5,2,128]{3,2,1,0:T(2,128)(2,1)S(1)} async-done(((bf16[64,5,2,128]{3,2,1,0:T(2,128)(2,1)}), bf16[64,5,2,128]{3,2,1,0:T(2,128)(2,1)S(1)}, u32[]{:S(2)}, u32[]{:S(2)}) %all-to-all-start) | async-done | bytes 163872 | tf_op jit(solution)/shard_map/all_to_all | solution.py:30
  33.9 0.0 copy-done.2
  33.9 0.0 copy-done.3
  33.9 2.0 %spans.1 = bf16[64,5,2,128]{3,2,1,0:T(2,128)(2,1)} custom-call(bf16[64,5,2,128]{3,2,1,0:T(2,128)(2,1)S(1)} %all-to-all-done.gathered_ref, f32[4,128]{1,0:T(4,128)S(1)} %copy-done.3, bf16[512,512]{1,0:T(8,128)(2,1)S(1)} %turn.1.keys_ref, bf16[4,512,128]{2,1,0:T(8,128)(2,1)S(1)} %copy-done.2), custom_call_target="tpu_custom_call" | custom-call | flops 536870912 | bytes 1572864 | tf_op jit(solution)/shard_map/spans/pallas_call | solution.py:318
  35.8 0.0 copy-start.1
  35.8 9.9 %all-to-all-start.1 = ((bf16[64,5,2,128]{3,2,1,0:T(2,128)(2,1)}), bf16[64,5,2,128]{3,2,1,0:T(2,128)(2,1)S(1)}, u32[]{:S(2)}, u32[]{:S(2)}) async-start(bf16[64,5,2,128]{3,2,1,0:T(2,128)(2,1)} %spans.1), calls=%async_computation.1 | async-start | bytes 327680 | tf_op jit(solution)/shard_map/all_to_all | solution.py:30
  45.7 0.0 copy-done.1
  45.8 0.1 fold.2
  45.9 2.7 %collective-permute-start.1 = (bf16[2,16,128]{2,1,0:T(8,128)(2,1)S(1)}, bf16[2,16,128]{2,1,0:T(8,128)(2,1)S(1)}, u32[]{:S(2)}, u32[]{:S(2)}) collective-permute-start(bf16[2,16,128]{2,1,0:T(8,128)(2,1)S(1)} %get-tuple-element.24), channel_id=1, source_target_pairs={{0,2},{1,3},{2,0},{3,1},{4,6},{5,7},{6,4},{7,5},{8,10},{9,11},{10,... | collective-permute-start | bytes 24584 | tf_op jit(solution)/shard_map/ppermute | solution.py:23
  48.6 2.8 %collective-permute-done.1.second_ref = bf16[2,16,128]{2,1,0:T(8,128)(2,1)S(1)} collective-permute-done((bf16[2,16,128]{2,1,0:T(8,128)(2,1)S(1)}, bf16[2,16,128]{2,1,0:T(8,128)(2,1)S(1)}, u32[]{:S(2)}, u32[]{:S(2)}) %collective-permute-start.1) | collective-permute-done | bytes 8224 | tf_op jit(solution)/shard_map/ppermute | solution.py:23
  51.4 0.1 fold.3
  51.5 2.4 %collective-permute-start.2 = (bf16[1,16,128]{2,1,0:T(8,128)(2,1)S(1)}, bf16[1,16,128]{2,1,0:T(8,128)(2,1)S(1)}, u32[]{:S(2)}, u32[]{:S(2)}) collective-permute-start(bf16[1,16,128]{2,1,0:T(8,128)(2,1)S(1)} %get-tuple-element.26), channel_id=1, source_target_pairs={{0,6},{1,7},{2,4},{3,5},{4,2},{5,3},{6,0},{7,1},{8,14},{9,15},{10,... | collective-permute-start | bytes 12296 | tf_op jit(solution)/shard_map/ppermute | solution.py:23
  53.9 4.3 %collective-permute-done.2.there_ref = bf16[1,16,128]{2,1,0:T(8,128)(2,1)S(1)} collective-permute-done((bf16[1,16,128]{2,1,0:T(8,128)(2,1)S(1)}, bf16[1,16,128]{2,1,0:T(8,128)(2,1)S(1)}, u32[]{:S(2)}, u32[]{:S(2)}) %collective-permute-start.2) | collective-permute-done | bytes 4128 | tf_op jit(solution)/shard_map/ppermute | solution.py:23
  58.2 0.0 all-to-all-done.1.spans_ref
  58.2 0.8 %merge.1 = bf16[1,1024]{1,0:T(2,128)(2,1)} custom-call(bf16[64,5,2,128]{3,2,1,0:T(2,128)(2,1)S(1)} %all-to-all-done.1.spans_ref, bf16[1,16,128]{2,1,0:T(8,128)(2,1)S(1)} %get-tuple-element.25.here_ref, bf16[1,16,128]{2,1,0:T(8,128)(2,1)S(1)} %collective-permute-done.2.there_ref), custom_call_target="tpu_custom_call" | custom-call | tf_op jit(solution)/shard_map/merge/pallas_call | solution.py:335
Async XLA Ops:
  1.4 32.4 %all-to-all-start = ((bf16[64,5,2,128]{3,2,1,0:T(2,128)(2,1)}), bf16[64,5,2,128]{3,2,1,0:T(2,128)(2,1)S(1)}, u32[]{:S(2)}, u32[]{:S(2)}) async-start(bf16[64,5,2,128]{3,2,1,0:T(2,128)(2,1)} %pack.1), calls=%async_computation | async-start | bytes 327680 | tf_op jit(solution)/shard_map/all_to_all | solution.py:30
  21.2 4.8 %copy-start = (bf16[4,512,128]{2,1,0:T(8,128)(2,1)S(1)}, bf16[4,512,128]{2,1,0:T(8,128)(2,1)}, u32[]{:S(2)}) copy-start(bf16[4,512,128]{2,1,0:T(8,128)(2,1)} %keys_ref) | copy-start | bytes 1572868
  23.9 10.0 %copy-start.2 = (bf16[4,512,128]{2,1,0:T(8,128)(2,1)S(1)}, bf16[4,512,128]{2,1,0:T(8,128)(2,1)}, u32[]{:S(2)}) copy-start(bf16[4,512,128]{2,1,0:T(8,128)(2,1)} %values_ref.1) | copy-start | bytes 1572868
  23.9 10.0 %copy-start.3 = (f32[4,128]{1,0:T(4,128)S(1)}, f32[4,128]{1,0:T(4,128)}, u32[]{:S(2)}) copy-start(f32[4,128]{1,0:T(4,128)} %get-tuple-element.19.idents_ref) | copy-start | bytes 6148
  23.9 3.4 %collective-permute-start = (bf16[4,16,128]{2,1,0:T(8,128)(2,1)}, bf16[4,16,128]{2,1,0:T(8,128)(2,1)S(1)}, u32[]{:S(2)}, u32[]{:S(2)}) collective-permute-start(bf16[4,16,128]{2,1,0:T(8,128)(2,1)} %get-tuple-element.17), channel_id=1, source_target_pairs={{0,1},{1,0},{2,3},{3,2},{4,5},{5,4},{6,7},{7,6},{8,9},{9,8},{10,11... | collective-permute-start | bytes 49160 | tf_op jit(solution)/shard_map/ppermute | solution.py:23
  35.8 9.9 %copy-start.1 = (bf16[4,16,128]{2,1,0:T(8,128)(2,1)S(1)}, bf16[4,16,128]{2,1,0:T(8,128)(2,1)}, u32[]{:S(2)}) copy-start(bf16[4,16,128]{2,1,0:T(8,128)(2,1)} %get-tuple-element.21.first_ref) | copy-start | bytes 49156
  35.8 22.4 %all-to-all-start.1 = ((bf16[64,5,2,128]{3,2,1,0:T(2,128)(2,1)}), bf16[64,5,2,128]{3,2,1,0:T(2,128)(2,1)S(1)}, u32[]{:S(2)}, u32[]{:S(2)}) async-start(bf16[64,5,2,128]{3,2,1,0:T(2,128)(2,1)} %spans.1), calls=%async_computation.1 | async-start | bytes 327680 | tf_op jit(solution)/shard_map/all_to_all | solution.py:30
  45.9 5.5 %collective-permute-start.1 = (bf16[2,16,128]{2,1,0:T(8,128)(2,1)S(1)}, bf16[2,16,128]{2,1,0:T(8,128)(2,1)S(1)}, u32[]{:S(2)}, u32[]{:S(2)}) collective-permute-start(bf16[2,16,128]{2,1,0:T(8,128)(2,1)S(1)} %get-tuple-element.24), channel_id=1, source_target_pairs={{0,2},{1,3},{2,0},{3,1},{4,6},{5,7},{6,4},{7,5},{8,10},{9,11},{10,... | collective-permute-start | bytes 24584 | tf_op jit(solution)/shard_map/ppermute | solution.py:23
  51.5 6.7 %collective-permute-start.2 = (bf16[1,16,128]{2,1,0:T(8,128)(2,1)S(1)}, bf16[1,16,128]{2,1,0:T(8,128)(2,1)S(1)}, u32[]{:S(2)}, u32[]{:S(2)}) collective-permute-start(bf16[1,16,128]{2,1,0:T(8,128)(2,1)S(1)} %get-tuple-element.26), channel_id=1, source_target_pairs={{0,6},{1,7},{2,4},{3,5},{4,2},{5,3},{6,0},{7,1},{8,14},{9,15},{10,... | collective-permute-start | bytes 12296 | tf_op jit(solution)/shard_map/ppermute | solution.py:23
